TPU v7x, 512 devices: a whole 4x4x16 slice. The times are simulated.
512 devices in a mesh: lat: 64 (over y_lo, z, core), lon: 8 (over y_hi, x).
Axes of the slice: x: 4, y: 4 (y_hi: 2, y_lo: 2; y = y_hi * 2 + y_lo), z: 16, core: 2. Of those that a mesh axis runs over, the one named last changes fastest.
Arguments:
- right_side: float32 [4, 4096, 7168], P(None, 'lat', 'lon'), may hold values from -8 to 8
- start: float32 [4, 4096, 7168], P(None, 'lat', 'lon'), may hold values from -8 to 8
- absorb: float32 [4, 4096, 7168], P(None, 'lat', 'lon'), may hold values from 0.05 to 1
- kappa_lat: float32 [4096, 7168], P('lat', 'lon'), may hold values from 0.2 to 5
- kappa_lon: float32 [4096, 7168], P('lat', 'lon'), may hold values from 0.2 to 5
Outputs:
- smoothed: float32 [4, 4096, 7168], P(None, 'lat', 'lon')
- residual: float32 [4, 4096, 7168], P(None, 'lat', 'lon')
All inputs are finite; a program needn't handle non-finite values.
Results may differ from a plain program's by a relative error of at most 0.00002.
Values sent between devices are 32-bit elements; how exact they have to be, the bound alone decides.
A program may use at most 64 MiB of HBM per device.

v0:
```python
import jax
import jax.numpy as jnp
from jax import lax
from jax.sharding import PartitionSpec as P

SWEEPS = 4


THETA = 1.05
DELTA = 0.95


def passed_along(value, axis, by):
    length = lax.axis_size(axis)
    return lax.ppermute(value, axis, [(i, (i + by) % length) for i in range(length)])


def padded_2(cells, sides, width, closed):
    for axis, dim in sides:
        count = lax.axis_size(axis)
        ends = count if closed else count - 1
        head = lax.slice_in_dim(cells, 0, width, axis=dim)
        tail = lax.slice_in_dim(cells, cells.shape[dim] - width, cells.shape[dim], axis=dim)
        cells = jnp.concatenate(
            [
                lax.ppermute(tail, axis, [(i, (i + 1) % count) for i in range(ends)]),
                cells,
                lax.ppermute(head, axis, [((i + 1) % count, i) for i in range(ends)]),
            ],
            axis=dim,
        )
    return cells


def neighbours(field):
    lat_index = lax.axis_index("lat")
    last_band = lax.axis_size("lat") - 1
    chosen = jnp.where(lat_index == 0, field[:, :1], field[:, -1:])
    opposite = passed_along(chosen, "lon", lax.axis_size("lon") // 2)
    padded = padded_2(field, (("lat", 1),), 1, False)
    above = jnp.where(lat_index == 0, opposite, padded[:, :1])
    below = jnp.where(lat_index == last_band, opposite, padded[:, -1:])
    north = jnp.concatenate([above, field[:, :-1]], axis=1)
    south = jnp.concatenate([field[:, 1:], below], axis=1)
    wrapped_cols = padded_2(field, (("lon", 2),), 1, True)
    west = wrapped_cols[:, :, :-2]
    east = wrapped_cols[:, :, 2:]
    return (north, south, west, east)


def on_device(right_side, start, absorb, kappa_lat, kappa_lon):
    kappas = jnp.stack([kappa_lat, kappa_lon])
    kap_n, kap_s, kap_w, kap_e = neighbours(kappas)
    c_north = 0.5 * (kappa_lat + kap_n[0])
    c_south = 0.5 * (kappa_lat + kap_s[0])
    c_west = 0.5 * (kappa_lon + kap_w[1])
    c_east = 0.5 * (kappa_lon + kap_e[1])
    diag = absorb + (c_north + c_south + c_west + c_east)
    sigma = THETA / DELTA
    rho = 1.0 / sigma

    def apply_op(field):
        north, south, west, east = neighbours(field)
        return diag * field - (c_north * north + c_south * south + c_west * west + c_east * east)

    state = start
    resid = right_side - apply_op(state)
    step_dir = resid / (THETA * diag)
    state = state + step_dir
    for sweep in range(SWEEPS - 1):
        resid = right_side - apply_op(state)
        rho_new = 1.0 / (2.0 * sigma - rho)
        step_dir = rho_new * rho * step_dir + 2.0 * rho_new / DELTA * (resid / diag)
        state = state + step_dir
        rho = rho_new
    return (state, right_side - apply_op(state))


def solution(mesh):
    return jax.shard_map(
        on_device,
        mesh=mesh,
        in_specs=(
            P(None, "lat", "lon"),
            P(None, "lat", "lon"),
            P(None, "lat", "lon"),
            P("lat", "lon"),
            P("lat", "lon"),
        ),
        out_specs=(P(None, "lat", "lon"), P(None, "lat", "lon")),
        check_vma=False,
    )
```

profile of v0, /device:TPU:14, one launch (start us, length us, event | category | flops | bytes accessed | tf_op | source)
XLA Modules:
  0.0 155.3 jit_solution(13984326993133237433)
XLA Ops:
  0.6 1.4 broadcast_select_fusion.17
  2.0 4.2 %collective-permute-start = (f32[2,1,896]{2,1,0:T(1,128)}, f32[2,1,896]{2,1,0:T(1,128)}, u32[]{:S(2)}, u32[]{:S(2)}) collective-permute-start(f32[2,1,896]{2,1,0:T(1,128)} %get-tuple-element.13), channel_id=1, source_target_pairs={{0,4},{1,5},{2,6},{3,7},{4,0},{5,1},{6,2},{7,3},{8,12},{9,13},{10,... | collective-permute-start | bytes 21512 | tf_op jit(solution)/shard_map/ppermute | solution.py:15
  6.2 1.9 %collective-permute-start.1 = (f32[2,1,896]{2,1,0:T(1,128)}, f32[2,1,896]{2,1,0:T(1,128)}, u32[]{:S(2)}, u32[]{:S(2)}) collective-permute-start(f32[2,1,896]{2,1,0:T(1,128)} %get-tuple-element.14), channel_id=1, source_target_pairs={{0,8},{8,16},{16,24},{24,32},{32,40},{40,48},{48,56},{56,64},{64,7... | collective-permute-start | bytes 21512 | tf_op jit(solution)/shard_map/ppermute | solution.py:26
  8.2 11.3 %collective-permute-start.2 = (f32[2,1,896]{2,1,0:T(1,128)}, f32[2,1,896]{2,1,0:T(1,128)}, u32[]{:S(2)}, u32[]{:S(2)}) collective-permute-start(f32[2,1,896]{2,1,0:T(1,128)} %get-tuple-element.15), channel_id=1, source_target_pairs={{8,0},{16,8},{24,16},{32,24},{40,32},{48,40},{56,48},{64,56},{72,6... | collective-permute-start | bytes 21512 | tf_op jit(solution)/shard_map/ppermute | solution.py:28
  19.5 1.6 %fusion.83 = (f32[4,1,896]{2,1,0:T(1,128)}, f32[4,1,896]{2,1,0:T(1,128)}, f32[4,1,896]{2,1,0:T(1,128)}) fusion(f32[4,64,896]{2,1,0:T(8,128)} %param.6, pred[]{:T(512)S(6)} %eq.4), kind=kLoop, calls=%fused_computation.130 | loop fusion | flops 3584 | bytes 71681 | tf_op jit(solution)/shard_map/slice | solution.py:38
  21.1 1.9 %collective-permute-start.6 = (f32[4,1,896]{2,1,0:T(1,128)}, f32[4,1,896]{2,1,0:T(1,128)S(1)}, u32[]{:S(2)}, u32[]{:S(2)}) collective-permute-start(f32[4,1,896]{2,1,0:T(1,128)} %get-tuple-element.44), channel_id=1, source_target_pairs={{0,8},{8,16},{16,24},{24,32},{32,40},{40,48},{48,56},{56,64},{64,7... | collective-permute-start | bytes 43016 | tf_op jit(solution)/shard_map/ppermute | solution.py:26
  23.1 5.9 %collective-permute-start.7 = (f32[4,1,896]{2,1,0:T(1,128)}, f32[4,1,896]{2,1,0:T(1,128)}, u32[]{:S(2)}, u32[]{:S(2)}) collective-permute-start(f32[4,1,896]{2,1,0:T(1,128)} %get-tuple-element.45), channel_id=1, source_target_pairs={{8,0},{16,8},{24,16},{32,24},{40,32},{48,40},{56,48},{64,56},{72,6... | collective-permute-start | bytes 43016 | tf_op jit(solution)/shard_map/ppermute | solution.py:28
  29.0 1.1 fusion.85
  30.1 1.0 fusion.47
  31.8 1.9 %collective-permute-start.5 = (f32[4,1,896]{2,1,0:T(1,128)}, f32[4,1,896]{2,1,0:T(1,128)S(1)}, u32[]{:S(2)}, u32[]{:S(2)}) collective-permute-start(f32[4,1,896]{2,1,0:T(1,128)} %get-tuple-element.46), channel_id=1, source_target_pairs={{0,4},{1,5},{2,6},{3,7},{4,0},{5,1},{6,2},{7,3},{8,12},{9,13},{10,... | collective-permute-start | bytes 43016 | tf_op jit(solution)/shard_map/ppermute | solution.py:15
  33.7 2.7 %collective-permute-start.4 = (f32[2,64,1]{2,1,0:T(8,128)}, f32[2,64,1]{2,1,0:T(8,128)S(1)}, u32[]{:S(2)}, u32[]{:S(2)}) collective-permute-start(f32[2,64,1]{2,1,0:T(8,128)} %get-tuple-element.51), channel_id=1, source_target_pairs={{1,0},{2,1},{3,2},{4,3},{5,4},{6,5},{7,6},{0,7},{9,8},{10,9},{11,1... | collective-permute-start | bytes 1544 | tf_op jit(solution)/shard_map/ppermute | solution.py:28
  36.5 6.7 %collective-permute-start.3 = (f32[2,64,1]{2,1,0:T(8,128)S(1)}, f32[2,64,1]{2,1,0:T(8,128)S(1)}, u32[]{:S(2)}, u32[]{:S(2)}) collective-permute-start(f32[2,64,1]{2,1,0:T(8,128)S(1)} %get-tuple-element.52), channel_id=1, source_target_pairs={{0,1},{1,2},{2,3},{3,4},{4,5},{5,6},{6,7},{7,0},{8,9},{9,10},{10,1... | collective-permute-start | bytes 1544 | tf_op jit(solution)/shard_map/ppermute | solution.py:26
  44.0 1.9 %collective-permute-start.8 = (f32[4,64,1]{2,1,0:T(8,128)S(1)}, f32[4,64,1]{2,1,0:T(8,128)S(1)}, u32[]{:S(2)}, u32[]{:S(2)}) collective-permute-start(f32[4,64,1]{2,1,0:T(8,128)S(1)} %get-tuple-element.49), channel_id=1, source_target_pairs={{0,1},{1,2},{2,3},{3,4},{4,5},{5,6},{6,7},{7,0},{8,9},{9,10},{10,1... | collective-permute-start | bytes 3080 | tf_op jit(solution)/shard_map/ppermute | solution.py:26
  45.9 3.9 %collective-permute-start.9 = (f32[4,64,1]{2,1,0:T(8,128)S(1)}, f32[4,64,1]{2,1,0:T(8,128)S(1)}, u32[]{:S(2)}, u32[]{:S(2)}) collective-permute-start(f32[4,64,1]{2,1,0:T(8,128)S(1)} %get-tuple-element.50), channel_id=1, source_target_pairs={{1,0},{2,1},{3,2},{4,3},{5,4},{6,5},{7,6},{0,7},{9,8},{10,9},{11,1... | collective-permute-start | bytes 3080 | tf_op jit(solution)/shard_map/ppermute | solution.py:28
  49.9 1.4 add_add_fusion
  52.1 4.3 %collective-permute-done.9 = f32[4,64,1]{2,1,0:T(8,128)S(1)} collective-permute-done((f32[4,64,1]{2,1,0:T(8,128)S(1)}, f32[4,64,1]{2,1,0:T(8,128)S(1)}, u32[]{:S(2)}, u32[]{:S(2)}) %collective-permute-start.9) | collective-permute-done | bytes 1056 | tf_op jit(solution)/shard_map/ppermute | solution.py:28
  57.4 1.9 %collective-permute-start.11 = (f32[4,1,896]{2,1,0:T(1,128)S(1)}, f32[4,1,896]{2,1,0:T(1,128)S(1)}, u32[]{:S(2)}, u32[]{:S(2)}) collective-permute-start(f32[4,1,896]{2,1,0:T(1,128)S(1)} %get-tuple-element.37), channel_id=1, source_target_pairs={{0,8},{8,16},{16,24},{24,32},{32,40},{40,48},{48,56},{56,64},{64,7... | collective-permute-start | bytes 43016 | tf_op jit(solution)/shard_map/ppermute | solution.py:26
  59.3 5.4 %collective-permute-start.10 = (f32[4,1,896]{2,1,0:T(1,128)S(1)}, f32[4,1,896]{2,1,0:T(1,128)S(1)}, u32[]{:S(2)}, u32[]{:S(2)}) collective-permute-start(f32[4,1,896]{2,1,0:T(1,128)S(1)} %get-tuple-element.38), channel_id=1, source_target_pairs={{0,4},{1,5},{2,6},{3,7},{4,0},{5,1},{6,2},{7,3},{8,12},{9,13},{10,... | collective-permute-start | bytes 43016 | tf_op jit(solution)/shard_map/ppermute | solution.py:15
  64.8 6.1 %collective-permute-start.12 = (f32[4,1,896]{2,1,0:T(1,128)S(1)}, f32[4,1,896]{2,1,0:T(1,128)S(1)}, u32[]{:S(2)}, u32[]{:S(2)}) collective-permute-start(f32[4,1,896]{2,1,0:T(1,128)S(1)} %get-tuple-element.39), channel_id=1, source_target_pairs={{8,0},{16,8},{24,16},{32,24},{40,32},{48,40},{56,48},{64,56},{72,6... | collective-permute-start | bytes 43016 | tf_op jit(solution)/shard_map/ppermute | solution.py:28
  70.9 2.2 %collective-permute-start.13 = (f32[4,64,1]{2,1,0:T(8,128)S(1)}, f32[4,64,1]{2,1,0:T(8,128)S(1)}, u32[]{:S(2)}, u32[]{:S(2)}) collective-permute-start(f32[4,64,1]{2,1,0:T(8,128)S(1)} %get-tuple-element.42), channel_id=1, source_target_pairs={{0,1},{1,2},{2,3},{3,4},{4,5},{5,6},{6,7},{7,0},{8,9},{9,10},{10,1... | collective-permute-start | bytes 3080 | tf_op jit(solution)/shard_map/ppermute | solution.py:26
  73.2 3.6 %collective-permute-start.14 = (f32[4,64,1]{2,1,0:T(8,128)S(1)}, f32[4,64,1]{2,1,0:T(8,128)S(1)}, u32[]{:S(2)}, u32[]{:S(2)}) collective-permute-start(f32[4,64,1]{2,1,0:T(8,128)S(1)} %get-tuple-element.43), channel_id=1, source_target_pairs={{1,0},{2,1},{3,2},{4,3},{5,4},{6,5},{7,6},{0,7},{9,8},{10,9},{11,1... | collective-permute-start | bytes 3080 | tf_op jit(solution)/shard_map/ppermute | solution.py:28
  76.9 0.9 collective-permute-done.13
  77.8 5.9 %collective-permute-done.14 = f32[4,64,1]{2,1,0:T(8,128)S(1)} collective-permute-done((f32[4,64,1]{2,1,0:T(8,128)S(1)}, f32[4,64,1]{2,1,0:T(8,128)S(1)}, u32[]{:S(2)}, u32[]{:S(2)}) %collective-permute-start.14) | collective-permute-done | bytes 1056 | tf_op jit(solution)/shard_map/ppermute | solution.py:28
  83.7 0.8 fusion.63
  84.7 1.9 %collective-permute-start.16 = (f32[4,1,896]{2,1,0:T(1,128)S(1)}, f32[4,1,896]{2,1,0:T(1,128)S(1)}, u32[]{:S(2)}, u32[]{:S(2)}) collective-permute-start(f32[4,1,896]{2,1,0:T(1,128)S(1)} %get-tuple-element.30), channel_id=1, source_target_pairs={{0,8},{8,16},{16,24},{24,32},{32,40},{40,48},{48,56},{56,64},{64,7... | collective-permute-start | bytes 43016 | tf_op jit(solution)/shard_map/ppermute | solution.py:26
  86.6 3.1 %collective-permute-start.15 = (f32[4,1,896]{2,1,0:T(1,128)S(1)}, f32[4,1,896]{2,1,0:T(1,128)S(1)}, u32[]{:S(2)}, u32[]{:S(2)}) collective-permute-start(f32[4,1,896]{2,1,0:T(1,128)S(1)} %get-tuple-element.31), channel_id=1, source_target_pairs={{0,4},{1,5},{2,6},{3,7},{4,0},{5,1},{6,2},{7,3},{8,12},{9,13},{10,... | collective-permute-start | bytes 43016 | tf_op jit(solution)/shard_map/ppermute | solution.py:15
  89.7 6.1 %collective-permute-start.17 = (f32[4,1,896]{2,1,0:T(1,128)S(1)}, f32[4,1,896]{2,1,0:T(1,128)S(1)}, u32[]{:S(2)}, u32[]{:S(2)}) collective-permute-start(f32[4,1,896]{2,1,0:T(1,128)S(1)} %get-tuple-element.32), channel_id=1, source_target_pairs={{8,0},{16,8},{24,16},{32,24},{40,32},{48,40},{56,48},{64,56},{72,6... | collective-permute-start | bytes 43016 | tf_op jit(solution)/shard_map/ppermute | solution.py:28
  95.9 1.9 %collective-permute-start.18 = (f32[4,64,1]{2,1,0:T(8,128)S(1)}, f32[4,64,1]{2,1,0:T(8,128)S(1)}, u32[]{:S(2)}, u32[]{:S(2)}) collective-permute-start(f32[4,64,1]{2,1,0:T(8,128)S(1)} %get-tuple-element.35), channel_id=1, source_target_pairs={{0,1},{1,2},{2,3},{3,4},{4,5},{5,6},{6,7},{7,0},{8,9},{9,10},{10,1... | collective-permute-start | bytes 3080 | tf_op jit(solution)/shard_map/ppermute | solution.py:26
  97.8 3.9 %collective-permute-start.19 = (f32[4,64,1]{2,1,0:T(8,128)S(1)}, f32[4,64,1]{2,1,0:T(8,128)S(1)}, u32[]{:S(2)}, u32[]{:S(2)}) collective-permute-start(f32[4,64,1]{2,1,0:T(8,128)S(1)} %get-tuple-element.36), channel_id=1, source_target_pairs={{1,0},{2,1},{3,2},{4,3},{5,4},{6,5},{7,6},{0,7},{9,8},{10,9},{11,1... | collective-permute-start | bytes 3080 | tf_op jit(solution)/shard_map/ppermute | solution.py:28
  101.8 0.9 collective-permute-done.18
  102.8 5.5 %collective-permute-done.19 = f32[4,64,1]{2,1,0:T(8,128)S(1)} collective-permute-done((f32[4,64,1]{2,1,0:T(8,128)S(1)}, f32[4,64,1]{2,1,0:T(8,128)S(1)}, u32[]{:S(2)}, u32[]{:S(2)}) %collective-permute-start.19) | collective-permute-done | bytes 1056 | tf_op jit(solution)/shard_map/ppermute | solution.py:28
  108.3 0.8 fusion.61
  109.3 1.9 %collective-permute-start.22 = (f32[4,1,896]{2,1,0:T(1,128)S(1)}, f32[4,1,896]{2,1,0:T(1,128)S(1)}, u32[]{:S(2)}, u32[]{:S(2)}) collective-permute-start(f32[4,1,896]{2,1,0:T(1,128)S(1)} %get-tuple-element.25), channel_id=1, source_target_pairs={{8,0},{16,8},{24,16},{32,24},{40,32},{48,40},{56,48},{64,56},{72,6... | collective-permute-start | bytes 43016 | tf_op jit(solution)/shard_map/ppermute | solution.py:28
  111.3 3.8 %collective-permute-start.20 = (f32[4,1,896]{2,1,0:T(1,128)S(1)}, f32[4,1,896]{2,1,0:T(1,128)S(1)}, u32[]{:S(2)}, u32[]{:S(2)}) collective-permute-start(f32[4,1,896]{2,1,0:T(1,128)S(1)} %get-tuple-element.26), channel_id=1, source_target_pairs={{0,4},{1,5},{2,6},{3,7},{4,0},{5,1},{6,2},{7,3},{8,12},{9,13},{10,... | collective-permute-start | bytes 43016 | tf_op jit(solution)/shard_map/ppermute | solution.py:15
  115.1 2.1 %collective-permute-start.21 = (f32[4,1,896]{2,1,0:T(1,128)S(1)}, f32[4,1,896]{2,1,0:T(1,128)S(1)}, u32[]{:S(2)}, u32[]{:S(2)}) collective-permute-start(f32[4,1,896]{2,1,0:T(1,128)S(1)} %get-tuple-element.27), channel_id=1, source_target_pairs={{0,8},{8,16},{16,24},{24,32},{32,40},{40,48},{48,56},{56,64},{64,7... | collective-permute-start | bytes 43016 | tf_op jit(solution)/shard_map/ppermute | solution.py:26
  117.3 1.9 %collective-permute-start.23 = (f32[4,64,1]{2,1,0:T(8,128)S(1)}, f32[4,64,1]{2,1,0:T(8,128)S(1)}, u32[]{:S(2)}, u32[]{:S(2)}) collective-permute-start(f32[4,64,1]{2,1,0:T(8,128)S(1)} %get-tuple-element.28), channel_id=1, source_target_pairs={{0,1},{1,2},{2,3},{3,4},{4,5},{5,6},{6,7},{7,0},{8,9},{9,10},{10,1... | collective-permute-start | bytes 3080 | tf_op jit(solution)/shard_map/ppermute | solution.py:26
  119.2 3.9 %collective-permute-start.24 = (f32[4,64,1]{2,1,0:T(8,128)S(1)}, f32[4,64,1]{2,1,0:T(8,128)S(1)}, u32[]{:S(2)}, u32[]{:S(2)}) collective-permute-start(f32[4,64,1]{2,1,0:T(8,128)S(1)} %get-tuple-element.29), channel_id=1, source_target_pairs={{1,0},{2,1},{3,2},{4,3},{5,4},{6,5},{7,6},{0,7},{9,8},{10,9},{11,1... | collective-permute-start | bytes 3080 | tf_op jit(solution)/shard_map/ppermute | solution.py:28
  123.2 1.4 collective-permute-done.23
  124.6 5.5 %collective-permute-done.24 = f32[4,64,1]{2,1,0:T(8,128)S(1)} collective-permute-done((f32[4,64,1]{2,1,0:T(8,128)S(1)}, f32[4,64,1]{2,1,0:T(8,128)S(1)}, u32[]{:S(2)}, u32[]{:S(2)}) %collective-permute-start.24) | collective-permute-done | bytes 1056 | tf_op jit(solution)/shard_map/ppermute | solution.py:28
  130.1 0.9 fusion.13
  131.2 4.0 %collective-permute-start.27 = (f32[4,1,896]{2,1,0:T(1,128)S(1)}, f32[4,1,896]{2,1,0:T(1,128)S(1)}, u32[]{:S(2)}, u32[]{:S(2)}) collective-permute-start(f32[4,1,896]{2,1,0:T(1,128)S(1)} %get-tuple-element.18), channel_id=1, source_target_pairs={{8,0},{16,8},{24,16},{32,24},{40,32},{48,40},{56,48},{64,56},{72,6... | collective-permute-start | bytes 43016 | tf_op jit(solution)/shard_map/ppermute | solution.py:28
  135.2 3.6 %collective-permute-start.25 = (f32[4,1,896]{2,1,0:T(1,128)S(1)}, f32[4,1,896]{2,1,0:T(1,128)S(1)}, u32[]{:S(2)}, u32[]{:S(2)}) collective-permute-start(f32[4,1,896]{2,1,0:T(1,128)S(1)} %get-tuple-element.19), channel_id=1, source_target_pairs={{0,4},{1,5},{2,6},{3,7},{4,0},{5,1},{6,2},{7,3},{8,12},{9,13},{10,... | collective-permute-start | bytes 43016 | tf_op jit(solution)/shard_map/ppermute | solution.py:15
  138.8 1.9 %collective-permute-start.26 = (f32[4,1,896]{2,1,0:T(1,128)S(1)}, f32[4,1,896]{2,1,0:T(1,128)S(1)}, u32[]{:S(2)}, u32[]{:S(2)}) collective-permute-start(f32[4,1,896]{2,1,0:T(1,128)S(1)} %get-tuple-element.20), channel_id=1, source_target_pairs={{0,8},{8,16},{16,24},{24,32},{32,40},{40,48},{48,56},{56,64},{64,7... | collective-permute-start | bytes 43016 | tf_op jit(solution)/shard_map/ppermute | solution.py:26
  140.8 2.4 %collective-permute-start.28 = (f32[4,64,1]{2,1,0:T(8,128)S(1)}, f32[4,64,1]{2,1,0:T(8,128)S(1)}, u32[]{:S(2)}, u32[]{:S(2)}) collective-permute-start(f32[4,64,1]{2,1,0:T(8,128)S(1)} %get-tuple-element.21), channel_id=1, source_target_pairs={{0,1},{1,2},{2,3},{3,4},{4,5},{5,6},{6,7},{7,0},{8,9},{9,10},{10,1... | collective-permute-start | bytes 3080 | tf_op jit(solution)/shard_map/ppermute | solution.py:26
  143.2 3.5 %collective-permute-start.29 = (f32[4,64,1]{2,1,0:T(8,128)S(1)}, f32[4,64,1]{2,1,0:T(8,128)S(1)}, u32[]{:S(2)}, u32[]{:S(2)}) collective-permute-start(f32[4,64,1]{2,1,0:T(8,128)S(1)} %get-tuple-element.22), channel_id=1, source_target_pairs={{1,0},{2,1},{3,2},{4,3},{5,4},{6,5},{7,6},{0,7},{9,8},{10,9},{11,1... | collective-permute-start | bytes 3080 | tf_op jit(solution)/shard_map/ppermute | solution.py:28
  146.7 0.9 collective-permute-done.28
  147.6 6.0 %collective-permute-done.29 = f32[4,64,1]{2,1,0:T(8,128)S(1)} collective-permute-done((f32[4,64,1]{2,1,0:T(8,128)S(1)}, f32[4,64,1]{2,1,0:T(8,128)S(1)}, u32[]{:S(2)}, u32[]{:S(2)}) %collective-permute-start.29) | collective-permute-done | bytes 1056 | tf_op jit(solution)/shard_map/ppermute | solution.py:28
  153.7 1.6 %fusion.3 = f32[4,64,896]{2,1,0:T(8,128)} fusion(f32[4,64,896]{2,1,0:T(8,128)S(1)} %copy-done, f32[4,64,1]{2,1,0:T(8,128)S(1)} %collective-permute-done.29, f32[4,64,896]{2,1,0:T(8,128)S(1)} %fusion.13, f32[4,64,1]{2,1,0:T(8,128)S(1)} %collective-permute-done.28, f32[4,63,896]{2,1,0:T(8,128)S(1)} %get-tuple-element.17, ...), kind=kLoop, calls=%fused_computation.4 | loop fusion | flops 3440640 | bytes 6653952 | tf_op jit(solution)/shard_map/sub | solution.py:76
  (54 shorter events, 4.3 us)
Async XLA Ops:
  2.0 29.8 %collective-permute-start = (f32[2,1,896]{2,1,0:T(1,128)}, f32[2,1,896]{2,1,0:T(1,128)}, u32[]{:S(2)}, u32[]{:S(2)}) collective-permute-start(f32[2,1,896]{2,1,0:T(1,128)} %get-tuple-element.13), channel_id=1, source_target_pairs={{0,4},{1,5},{2,6},{3,7},{4,0},{5,1},{6,2},{7,3},{8,12},{9,13},{10,... | collective-permute-start | bytes 21512 | tf_op jit(solution)/shard_map/ppermute | solution.py:15
  6.2 27.5 %collective-permute-start.1 = (f32[2,1,896]{2,1,0:T(1,128)}, f32[2,1,896]{2,1,0:T(1,128)}, u32[]{:S(2)}, u32[]{:S(2)}) collective-permute-start(f32[2,1,896]{2,1,0:T(1,128)} %get-tuple-element.14), channel_id=1, source_target_pairs={{0,8},{8,16},{16,24},{24,32},{32,40},{40,48},{48,56},{56,64},{64,7... | collective-permute-start | bytes 21512 | tf_op jit(solution)/shard_map/ppermute | solution.py:26
  8.2 28.3 %collective-permute-start.2 = (f32[2,1,896]{2,1,0:T(1,128)}, f32[2,1,896]{2,1,0:T(1,128)}, u32[]{:S(2)}, u32[]{:S(2)}) collective-permute-start(f32[2,1,896]{2,1,0:T(1,128)} %get-tuple-element.15), channel_id=1, source_target_pairs={{8,0},{16,8},{24,16},{32,24},{40,32},{48,40},{56,48},{64,56},{72,6... | collective-permute-start | bytes 21512 | tf_op jit(solution)/shard_map/ppermute | solution.py:28
  21.1 30.1 %collective-permute-start.6 = (f32[4,1,896]{2,1,0:T(1,128)}, f32[4,1,896]{2,1,0:T(1,128)S(1)}, u32[]{:S(2)}, u32[]{:S(2)}) collective-permute-start(f32[4,1,896]{2,1,0:T(1,128)} %get-tuple-element.44), channel_id=1, source_target_pairs={{0,8},{8,16},{16,24},{24,32},{32,40},{40,48},{48,56},{56,64},{64,7... | collective-permute-start | bytes 43016 | tf_op jit(solution)/shard_map/ppermute | solution.py:26
  23.0 7.0 %copy-start.4 = (f32[64,896]{1,0:T(8,128)S(1)}, f32[64,896]{1,0:T(8,128)}, u32[]{:S(2)}) copy-start(f32[64,896]{1,0:T(8,128)} %param.8) | copy-start | bytes 688132
  23.1 7.0 %copy-start.5 = (f32[64,896]{1,0:T(8,128)S(1)}, f32[64,896]{1,0:T(8,128)}, u32[]{:S(2)}) copy-start(f32[64,896]{1,0:T(8,128)} %param.9) | copy-start | bytes 688132
  23.1 8.0 %copy-start.3 = (f32[4,64,896]{2,1,0:T(8,128)S(1)}, f32[4,64,896]{2,1,0:T(8,128)}, u32[]{:S(2)}) copy-start(f32[4,64,896]{2,1,0:T(8,128)} %param.6) | copy-start | bytes 2752516
  23.1 28.2 %collective-permute-start.7 = (f32[4,1,896]{2,1,0:T(1,128)}, f32[4,1,896]{2,1,0:T(1,128)}, u32[]{:S(2)}, u32[]{:S(2)}) collective-permute-start(f32[4,1,896]{2,1,0:T(1,128)} %get-tuple-element.45), channel_id=1, source_target_pairs={{8,0},{16,8},{24,16},{32,24},{40,32},{48,40},{56,48},{64,56},{72,6... | collective-permute-start | bytes 43016 | tf_op jit(solution)/shard_map/ppermute | solution.py:28
  31.8 19.5 %collective-permute-start.5 = (f32[4,1,896]{2,1,0:T(1,128)}, f32[4,1,896]{2,1,0:T(1,128)S(1)}, u32[]{:S(2)}, u32[]{:S(2)}) collective-permute-start(f32[4,1,896]{2,1,0:T(1,128)} %get-tuple-element.46), channel_id=1, source_target_pairs={{0,4},{1,5},{2,6},{3,7},{4,0},{5,1},{6,2},{7,3},{8,12},{9,13},{10,... | collective-permute-start | bytes 43016 | tf_op jit(solution)/shard_map/ppermute | solution.py:15
  33.7 10.2 %collective-permute-start.4 = (f32[2,64,1]{2,1,0:T(8,128)}, f32[2,64,1]{2,1,0:T(8,128)S(1)}, u32[]{:S(2)}, u32[]{:S(2)}) collective-permute-start(f32[2,64,1]{2,1,0:T(8,128)} %get-tuple-element.51), channel_id=1, source_target_pairs={{1,0},{2,1},{3,2},{4,3},{5,4},{6,5},{7,6},{0,7},{9,8},{10,9},{11,1... | collective-permute-start | bytes 1544 | tf_op jit(solution)/shard_map/ppermute | solution.py:28
  36.5 9.4 %collective-permute-start.3 = (f32[2,64,1]{2,1,0:T(8,128)S(1)}, f32[2,64,1]{2,1,0:T(8,128)S(1)}, u32[]{:S(2)}, u32[]{:S(2)}) collective-permute-start(f32[2,64,1]{2,1,0:T(8,128)S(1)} %get-tuple-element.52), channel_id=1, source_target_pairs={{0,1},{1,2},{2,3},{3,4},{4,5},{5,6},{6,7},{7,0},{8,9},{9,10},{10,1... | collective-permute-start | bytes 1544 | tf_op jit(solution)/shard_map/ppermute | solution.py:26
  44.0 8.1 %collective-permute-start.8 = (f32[4,64,1]{2,1,0:T(8,128)S(1)}, f32[4,64,1]{2,1,0:T(8,128)S(1)}, u32[]{:S(2)}, u32[]{:S(2)}) collective-permute-start(f32[4,64,1]{2,1,0:T(8,128)S(1)} %get-tuple-element.49), channel_id=1, source_target_pairs={{0,1},{1,2},{2,3},{3,4},{4,5},{5,6},{6,7},{7,0},{8,9},{9,10},{10,1... | collective-permute-start | bytes 3080 | tf_op jit(solution)/shard_map/ppermute | solution.py:26
  45.9 10.5 %collective-permute-start.9 = (f32[4,64,1]{2,1,0:T(8,128)S(1)}, f32[4,64,1]{2,1,0:T(8,128)S(1)}, u32[]{:S(2)}, u32[]{:S(2)}) collective-permute-start(f32[4,64,1]{2,1,0:T(8,128)S(1)} %get-tuple-element.50), channel_id=1, source_target_pairs={{1,0},{2,1},{3,2},{4,3},{5,4},{6,5},{7,6},{0,7},{9,8},{10,9},{11,1... | collective-permute-start | bytes 3080 | tf_op jit(solution)/shard_map/ppermute | solution.py:28
  49.9 6.5 %copy-start = (f32[4,64,896]{2,1,0:T(8,128)S(1)}, f32[4,64,896]{2,1,0:T(8,128)}, u32[]{:S(2)}) copy-start(f32[4,64,896]{2,1,0:T(8,128)} %param.5) | copy-start | bytes 2752516
  49.9 6.5 %copy-start.1 = (f32[4,64,896]{2,1,0:T(8,128)S(1)}, f32[4,64,896]{2,1,0:T(8,128)}, u32[]{:S(2)}) copy-start(f32[4,64,896]{2,1,0:T(8,128)} %param.7) | copy-start | bytes 2752516
  57.4 19.4 %collective-permute-start.11 = (f32[4,1,896]{2,1,0:T(1,128)S(1)}, f32[4,1,896]{2,1,0:T(1,128)S(1)}, u32[]{:S(2)}, u32[]{:S(2)}) collective-permute-start(f32[4,1,896]{2,1,0:T(1,128)S(1)} %get-tuple-element.37), channel_id=1, source_target_pairs={{0,8},{8,16},{16,24},{24,32},{32,40},{40,48},{48,56},{56,64},{64,7... | collective-permute-start | bytes 43016 | tf_op jit(solution)/shard_map/ppermute | solution.py:26
  59.3 17.5 %collective-permute-start.10 = (f32[4,1,896]{2,1,0:T(1,128)S(1)}, f32[4,1,896]{2,1,0:T(1,128)S(1)}, u32[]{:S(2)}, u32[]{:S(2)}) collective-permute-start(f32[4,1,896]{2,1,0:T(1,128)S(1)} %get-tuple-element.38), channel_id=1, source_target_pairs={{0,4},{1,5},{2,6},{3,7},{4,0},{5,1},{6,2},{7,3},{8,12},{9,13},{10,... | collective-permute-start | bytes 43016 | tf_op jit(solution)/shard_map/ppermute | solution.py:15
  64.8 12.1 %collective-permute-start.12 = (f32[4,1,896]{2,1,0:T(1,128)S(1)}, f32[4,1,896]{2,1,0:T(1,128)S(1)}, u32[]{:S(2)}, u32[]{:S(2)}) collective-permute-start(f32[4,1,896]{2,1,0:T(1,128)S(1)} %get-tuple-element.39), channel_id=1, source_target_pairs={{8,0},{16,8},{24,16},{32,24},{40,32},{48,40},{56,48},{64,56},{72,6... | collective-permute-start | bytes 43016 | tf_op jit(solution)/shard_map/ppermute | solution.py:28
  70.9 6.9 %collective-permute-start.13 = (f32[4,64,1]{2,1,0:T(8,128)S(1)}, f32[4,64,1]{2,1,0:T(8,128)S(1)}, u32[]{:S(2)}, u32[]{:S(2)}) collective-permute-start(f32[4,64,1]{2,1,0:T(8,128)S(1)} %get-tuple-element.42), channel_id=1, source_target_pairs={{0,1},{1,2},{2,3},{3,4},{4,5},{5,6},{6,7},{7,0},{8,9},{9,10},{10,1... | collective-permute-start | bytes 3080 | tf_op jit(solution)/shard_map/ppermute | solution.py:26
  73.2 10.5 %collective-permute-start.14 = (f32[4,64,1]{2,1,0:T(8,128)S(1)}, f32[4,64,1]{2,1,0:T(8,128)S(1)}, u32[]{:S(2)}, u32[]{:S(2)}) collective-permute-start(f32[4,64,1]{2,1,0:T(8,128)S(1)} %get-tuple-element.43), channel_id=1, source_target_pairs={{1,0},{2,1},{3,2},{4,3},{5,4},{6,5},{7,6},{0,7},{9,8},{10,9},{11,1... | collective-permute-start | bytes 3080 | tf_op jit(solution)/shard_map/ppermute | solution.py:28
  84.7 17.1 %collective-permute-start.16 = (f32[4,1,896]{2,1,0:T(1,128)S(1)}, f32[4,1,896]{2,1,0:T(1,128)S(1)}, u32[]{:S(2)}, u32[]{:S(2)}) collective-permute-start(f32[4,1,896]{2,1,0:T(1,128)S(1)} %get-tuple-element.30), channel_id=1, source_target_pairs={{0,8},{8,16},{16,24},{24,32},{32,40},{40,48},{48,56},{56,64},{64,7... | collective-permute-start | bytes 43016 | tf_op jit(solution)/shard_map/ppermute | solution.py:26
  86.6 15.2 %collective-permute-start.15 = (f32[4,1,896]{2,1,0:T(1,128)S(1)}, f32[4,1,896]{2,1,0:T(1,128)S(1)}, u32[]{:S(2)}, u32[]{:S(2)}) collective-permute-start(f32[4,1,896]{2,1,0:T(1,128)S(1)} %get-tuple-element.31), channel_id=1, source_target_pairs={{0,4},{1,5},{2,6},{3,7},{4,0},{5,1},{6,2},{7,3},{8,12},{9,13},{10,... | collective-permute-start | bytes 43016 | tf_op jit(solution)/shard_map/ppermute | solution.py:15
  89.7 12.1 %collective-permute-start.17 = (f32[4,1,896]{2,1,0:T(1,128)S(1)}, f32[4,1,896]{2,1,0:T(1,128)S(1)}, u32[]{:S(2)}, u32[]{:S(2)}) collective-permute-start(f32[4,1,896]{2,1,0:T(1,128)S(1)} %get-tuple-element.32), channel_id=1, source_target_pairs={{8,0},{16,8},{24,16},{32,24},{40,32},{48,40},{56,48},{64,56},{72,6... | collective-permute-start | bytes 43016 | tf_op jit(solution)/shard_map/ppermute | solution.py:28
  95.9 6.9 %collective-permute-start.18 = (f32[4,64,1]{2,1,0:T(8,128)S(1)}, f32[4,64,1]{2,1,0:T(8,128)S(1)}, u32[]{:S(2)}, u32[]{:S(2)}) collective-permute-start(f32[4,64,1]{2,1,0:T(8,128)S(1)} %get-tuple-element.35), channel_id=1, source_target_pairs={{0,1},{1,2},{2,3},{3,4},{4,5},{5,6},{6,7},{7,0},{8,9},{9,10},{10,1... | collective-permute-start | bytes 3080 | tf_op jit(solution)/shard_map/ppermute | solution.py:26
  97.8 10.5 %collective-permute-start.19 = (f32[4,64,1]{2,1,0:T(8,128)S(1)}, f32[4,64,1]{2,1,0:T(8,128)S(1)}, u32[]{:S(2)}, u32[]{:S(2)}) collective-permute-start(f32[4,64,1]{2,1,0:T(8,128)S(1)} %get-tuple-element.36), channel_id=1, source_target_pairs={{1,0},{2,1},{3,2},{4,3},{5,4},{6,5},{7,6},{0,7},{9,8},{10,9},{11,1... | collective-permute-start | bytes 3080 | tf_op jit(solution)/shard_map/ppermute | solution.py:28
  109.3 13.8 %collective-permute-start.22 = (f32[4,1,896]{2,1,0:T(1,128)S(1)}, f32[4,1,896]{2,1,0:T(1,128)S(1)}, u32[]{:S(2)}, u32[]{:S(2)}) collective-permute-start(f32[4,1,896]{2,1,0:T(1,128)S(1)} %get-tuple-element.25), channel_id=1, source_target_pairs={{8,0},{16,8},{24,16},{32,24},{40,32},{48,40},{56,48},{64,56},{72,6... | collective-permute-start | bytes 43016 | tf_op jit(solution)/shard_map/ppermute | solution.py:28
  111.3 11.9 %collective-permute-start.20 = (f32[4,1,896]{2,1,0:T(1,128)S(1)}, f32[4,1,896]{2,1,0:T(1,128)S(1)}, u32[]{:S(2)}, u32[]{:S(2)}) collective-permute-start(f32[4,1,896]{2,1,0:T(1,128)S(1)} %get-tuple-element.26), channel_id=1, source_target_pairs={{0,4},{1,5},{2,6},{3,7},{4,0},{5,1},{6,2},{7,3},{8,12},{9,13},{10,... | collective-permute-start | bytes 43016 | tf_op jit(solution)/shard_map/ppermute | solution.py:15
  115.1 8.1 %collective-permute-start.21 = (f32[4,1,896]{2,1,0:T(1,128)S(1)}, f32[4,1,896]{2,1,0:T(1,128)S(1)}, u32[]{:S(2)}, u32[]{:S(2)}) collective-permute-start(f32[4,1,896]{2,1,0:T(1,128)S(1)} %get-tuple-element.27), channel_id=1, source_target_pairs={{0,8},{8,16},{16,24},{24,32},{32,40},{40,48},{48,56},{56,64},{64,7... | collective-permute-start | bytes 43016 | tf_op jit(solution)/shard_map/ppermute | solution.py:26
  117.3 7.3 %collective-permute-start.23 = (f32[4,64,1]{2,1,0:T(8,128)S(1)}, f32[4,64,1]{2,1,0:T(8,128)S(1)}, u32[]{:S(2)}, u32[]{:S(2)}) collective-permute-start(f32[4,64,1]{2,1,0:T(8,128)S(1)} %get-tuple-element.28), channel_id=1, source_target_pairs={{0,1},{1,2},{2,3},{3,4},{4,5},{5,6},{6,7},{7,0},{8,9},{9,10},{10,1... | collective-permute-start | bytes 3080 | tf_op jit(solution)/shard_map/ppermute | solution.py:26
  119.2 10.9 %collective-permute-start.24 = (f32[4,64,1]{2,1,0:T(8,128)S(1)}, f32[4,64,1]{2,1,0:T(8,128)S(1)}, u32[]{:S(2)}, u32[]{:S(2)}) collective-permute-start(f32[4,64,1]{2,1,0:T(8,128)S(1)} %get-tuple-element.29), channel_id=1, source_target_pairs={{1,0},{2,1},{3,2},{4,3},{5,4},{6,5},{7,6},{0,7},{9,8},{10,9},{11,1... | collective-permute-start | bytes 3080 | tf_op jit(solution)/shard_map/ppermute | solution.py:28
  131.0 22.6 %copy-start.2 = (f32[4,64,896]{2,1,0:T(8,128)}, f32[4,64,896]{2,1,0:T(8,128)S(1)}, u32[]{:S(2)}) copy-start(f32[4,64,896]{2,1,0:T(8,128)S(1)} %fusion.13) | copy-start | bytes 2752516
  131.2 15.4 %collective-permute-start.27 = (f32[4,1,896]{2,1,0:T(1,128)S(1)}, f32[4,1,896]{2,1,0:T(1,128)S(1)}, u32[]{:S(2)}, u32[]{:S(2)}) collective-permute-start(f32[4,1,896]{2,1,0:T(1,128)S(1)} %get-tuple-element.18), channel_id=1, source_target_pairs={{8,0},{16,8},{24,16},{32,24},{40,32},{48,40},{56,48},{64,56},{72,6... | collective-permute-start | bytes 43016 | tf_op jit(solution)/shard_map/ppermute | solution.py:28
  135.2 11.5 %collective-permute-start.25 = (f32[4,1,896]{2,1,0:T(1,128)S(1)}, f32[4,1,896]{2,1,0:T(1,128)S(1)}, u32[]{:S(2)}, u32[]{:S(2)}) collective-permute-start(f32[4,1,896]{2,1,0:T(1,128)S(1)} %get-tuple-element.19), channel_id=1, source_target_pairs={{0,4},{1,5},{2,6},{3,7},{4,0},{5,1},{6,2},{7,3},{8,12},{9,13},{10,... | collective-permute-start | bytes 43016 | tf_op jit(solution)/shard_map/ppermute | solution.py:15
  138.8 7.9 %collective-permute-start.26 = (f32[4,1,896]{2,1,0:T(1,128)S(1)}, f32[4,1,896]{2,1,0:T(1,128)S(1)}, u32[]{:S(2)}, u32[]{:S(2)}) collective-permute-start(f32[4,1,896]{2,1,0:T(1,128)S(1)} %get-tuple-element.20), channel_id=1, source_target_pairs={{0,8},{8,16},{16,24},{24,32},{32,40},{40,48},{48,56},{56,64},{64,7... | collective-permute-start | bytes 43016 | tf_op jit(solution)/shard_map/ppermute | solution.py:26
  140.8 6.9 %collective-permute-start.28 = (f32[4,64,1]{2,1,0:T(8,128)S(1)}, f32[4,64,1]{2,1,0:T(8,128)S(1)}, u32[]{:S(2)}, u32[]{:S(2)}) collective-permute-start(f32[4,64,1]{2,1,0:T(8,128)S(1)} %get-tuple-element.21), channel_id=1, source_target_pairs={{0,1},{1,2},{2,3},{3,4},{4,5},{5,6},{6,7},{7,0},{8,9},{9,10},{10,1... | collective-permute-start | bytes 3080 | tf_op jit(solution)/shard_map/ppermute | solution.py:26
  143.2 10.5 %collective-permute-start.29 = (f32[4,64,1]{2,1,0:T(8,128)S(1)}, f32[4,64,1]{2,1,0:T(8,128)S(1)}, u32[]{:S(2)}, u32[]{:S(2)}) collective-permute-start(f32[4,64,1]{2,1,0:T(8,128)S(1)} %get-tuple-element.22), channel_id=1, source_target_pairs={{1,0},{2,1},{3,2},{4,3},{5,4},{6,5},{7,6},{0,7},{9,8},{10,9},{11,1... | collective-permute-start | bytes 3080 | tf_op jit(solution)/shard_map/ppermute | solution.py:28
where the time goes:
time: 156 us; the launch traced here: 155 us
  starting transfers between devices  108 us (69%)
  waiting for transfers between devices  31.5 us (20%)
  other arithmetic  12.8 us (8%)
  local copies, waits for them, and re-layouts  2.12 us (1%)
    ppermute x12, starting transfers between devices, padded_2(): lax.ppermute(head, axis, [((i + 1) % count, i) for i in range(ends)])  56.8 us
    ppermute x12, starting transfers between devices, padded_2(): lax.ppermute(tail, axis, [(i, (i + 1) % count) for i in range(ends)])  28.8 us
    ppermute x12, waiting for transfers between devices, padded_2(): lax.ppermute(head, axis, [((i + 1) % count, i) for i in range(ends)])  27.3 us
    ppermute x6, starting transfers between devices, passed_along(): lax.ppermute(value, axis, [(i, (i + by) % length) for i in range(length)])  22 us
    ppermute x12, waiting for transfers between devices, padded_2(): lax.ppermute(tail, axis, [(i, (i + 1) % count) for i in range(ends)])  4.2 us
    add x4, other arithmetic, on_device(): state = state + step_dir  3.4 us
  transfers between devices with their start and end apart: 30, of which 9 were waited for; matrix products, arithmetic and copies ran while one was open for 5% of the time, Pallas kernels for 0%

commit v1 on v0

v1 whole, which is shorter than its diff:
```python
import functools

import jax
import jax.numpy as jnp
from jax import lax
from jax.experimental import pallas as pl
from jax.experimental.pallas import tpu as pltpu
from jax.sharding import PartitionSpec as P

SWEEPS = 4
THETA = 1.05
DELTA = 0.95

MESH = pl.DeviceIdType.MESH
LANES = 128
REACH = 5
START, KLAT, KLON, RIGHT, ABSORB = 0, 4, 5, 6, 10
PLANES = 14
NORTH, SOUTH = 0, 1
OWN, EXTRA = 16, 8


def sweep_factors():
    sigma = THETA / DELTA
    rho = 1.0 / sigma
    factors = []
    for _ in range(SWEEPS - 1):
        rho_new = 1.0 / (2.0 * sigma - rho)
        factors.append((rho_new * rho, 2.0 * rho_new / DELTA))
        rho = rho_new
    return factors


def lane_of(shape):
    return lax.broadcasted_iota(jnp.int32, shape, len(shape) - 1)


def from_west(left, here):
    axis = here.ndim - 1
    return pltpu.roll(jnp.where(lane_of(here.shape) == LANES - 1, left, here), 1, axis)


def from_east(right, here):
    axis = here.ndim - 1
    return pltpu.roll(jnp.where(lane_of(here.shape) == 0, right, here), LANES - 1, axis)


def each_tile(count, body):
    def step(t, carry):
        body(t)
        return carry

    lax.fori_loop(0, count, step, 0)


class Region:
    def __init__(self, field, other, gain, scaled, coeff, tiles):
        self.field, self.other, self.gain, self.scaled, self.coeff, self.tiles = field, other, gain, scaled, coeff, tiles

    def around(self, t):
        return lax.rem(t + self.tiles - 1, self.tiles), lax.rem(t + 1, self.tiles)

    def coupling(self, x, t, first, cn, cs, cw, ce):
        west, east = self.around(t)
        rows = pl.ds(first, 8)
        here = x[0:4, t, rows, :]
        total = cn * x[0:4, t, pl.ds(first - 1, 8), :] + cs * x[0:4, t, pl.ds(first + 1, 8), :]
        total += cw * from_west(x[0:4, west, rows, :], here) + ce * from_east(x[0:4, east, rows, :], here)
        return here, total

    def opening(self, starts):
        def tile(t):
            west, east = self.around(t)
            for first in starts:
                rows = pl.ds(first, 8)
                kap = self.field[KLAT, t, rows, :]
                cn = 0.5 * (kap + self.field[KLAT, t, pl.ds(first - 1, 8), :])
                cs = 0.5 * (kap + self.field[KLAT, t, pl.ds(first + 1, 8), :])
                kap = self.field[KLON, t, rows, :]
                cw = 0.5 * (kap + from_west(self.field[KLON, west, rows, :], kap))
                ce = 0.5 * (kap + from_east(self.field[KLON, east, rows, :], kap))
                for place, value in enumerate((cn, cs, cw, ce)):
                    self.coeff[place, t, rows, :] = value
                gain = 1.0 / (self.field[ABSORB : ABSORB + 4, t, rows, :] + (cn + cs + cw + ce))
                scaled = self.field[RIGHT : RIGHT + 4, t, rows, :] * gain
                self.gain[:, t, rows, :] = gain
                self.scaled[:, t, rows, :] = scaled
                here, total = self.coupling(self.field, t, first, cn, cs, cw, ce)
                self.other[:, t, rows, :] = here + (scaled - here + gain * total) * (1.0 / THETA)

        each_tile(self.tiles, tile)

    def sweep(self, now, before, starts, keep, push):
        def tile(t):
            for first in starts:
                rows = pl.ds(first, 8)
                cn, cs, cw, ce = (self.coeff[place, t, rows, :] for place in range(4))
                here, total = self.coupling(now, t, first, cn, cs, cw, ce)
                change = push * (self.scaled[:, t, rows, :] + self.gain[:, t, rows, :] * total)
                before[0:4, t, rows, :] = (1.0 + keep - push) * here - keep * before[0:4, t, rows, :] + change

        each_tile(self.tiles, tile)

    def closing(self, x, starts, smoothed, residual, targets):
        def tile(t):
            columns = pl.ds(pl.multiple_of(t * LANES, LANES), LANES)
            for first, target in zip(starts, targets):
                rows = pl.ds(first, 8)
                cn, cs, cw, ce = (self.coeff[place, t, rows, :] for place in range(4))
                here, total = self.coupling(x, t, first, cn, cs, cw, ce)
                diag = self.field[ABSORB : ABSORB + 4, t, rows, :] + (cn + cs + cw + ce)
                smoothed[:, pl.ds(target, 8), columns] = here
                residual[:, pl.ds(target, 8), columns] = self.field[RIGHT : RIGHT + 4, t, rows, :] - (diag * here - total)

        each_tile(self.tiles - 1, tile)

    def run(self, starts, ends, smoothed, residual, targets):
        self.opening(starts)
        now, before = self.other, self.field
        for keep, push in sweep_factors():
            self.sweep(now, before, starts, keep, push)
            now, before = before, now
        self.closing(now, ends, smoothed, residual, targets)


def flipped(block):
    axis = block.ndim - 2
    row = lax.broadcasted_iota(jnp.int32, block.shape, axis)
    block = pltpu.roll(block, 4, axis)
    block = jnp.where((row & 2) == 0, pltpu.roll(block, 6, axis), pltpu.roll(block, 2, axis))
    return jnp.where((row & 1) == 0, pltpu.roll(block, 7, axis), pltpu.roll(block, 1, axis))


def kernel(
    bands, sectors, right_ref, start_ref, absorb_ref, klat_ref, klon_ref, smoothed, residual,
    field, other, gain, scaled, coeff,
    band_field, band_other, band_gain, band_scaled, band_coeff,
    to_west, to_east, east_in, west_in,
    load_sem, own_sem, row_send, row_recv, side_send, side_recv,
):
    rows = right_ref.shape[1]
    tiles = right_ref.shape[2] // LANES
    la, lo = lax.axis_index("lat"), lax.axis_index("lon")
    half = sectors // 2
    top, bottom = la == 0, la == bands - 1
    la_n = jnp.maximum(la - 1, 0)
    la_s = jnp.minimum(la + 1, bands - 1)
    lo_n = lo + jnp.where(top, half, 0)
    lo_s = lo + jnp.where(bottom, half, 0)

    def at(lat, lon):
        return (lat, lax.rem(lon + sectors, sectors))

    north, south, east, west = at(la_n, lo_n), at(la_s, lo_s), at(la, lo + 1), at(la, lo - 1)
    ne, nw, se, sw = at(la_n, lo_n + 1), at(la_n, lo_n - 1), at(la_s, lo_s + 1), at(la_s, lo_s - 1)

    barrier = pltpu.get_barrier_semaphore()
    for device in (north, south, east, west, ne, nw, se, sw):
        pl.semaphore_signal(barrier, inc=1, device_id=device, device_id_type=MESH)

    sources = ((start_ref, START, 4), (klat_ref, KLAT, 1), (klon_ref, KLON, 1), (right_ref, RIGHT, 4), (absorb_ref, ABSORB, 4))

    def load(t):
        columns = pl.ds(pl.multiple_of(t * LANES, LANES), LANES)
        for ref, plane, depth in sources:
            if depth == 1:
                src, dst = ref.at[:, columns], field.at[plane, t, pl.ds(8, rows), :]
            else:
                src, dst = ref.at[:, :, columns], field.at[plane : plane + 4, t, pl.ds(8, rows), :]
            pltpu.make_async_copy(src, dst, load_sem.at[t]).start()

    def loaded(t):
        whole = field.at[:, t, pl.ds(8, rows), :]
        pltpu.make_async_copy(whole, whole, load_sem.at[t]).wait()

    load(0)
    load(tiles - 1)
    lax.fori_loop(1, tiles - 1, lambda t, c: (load(t), c)[1], 0)
    pl.semaphore_wait(barrier, 8)

    def send_rows(way, device, band, from_top, into):
        def tile(t):
            columns = pl.ds(pl.multiple_of(t * LANES, LANES), LANES)
            for ref, plane, depth in sources:
                count = REACH if plane < KLON else REACH - 1
                first = 0 if from_top else rows - count
                group = 0 if plane < KLON else 1
                place = into if from_top else into + 8 - count
                if depth == 1:
                    src = ref.at[pl.ds(first, count), columns]
                    dst = band_field.at[band, plane, t, pl.ds(place, count), :]
                else:
                    src = ref.at[:, pl.ds(first, count), columns]
                    dst = band_field.at[band, plane : plane + 4, t, pl.ds(place, count), :]
                pltpu.make_async_remote_copy(
                    src_ref=src, dst_ref=dst, send_sem=row_send.at[way, group], recv_sem=row_recv.at[band, group],
                    device_id=device, device_id_type=MESH,
                ).start()

        each_tile(tiles, tile)

    pl.when(bottom)(lambda: send_rows(SOUTH, south, SOUTH, False, OWN))
    pl.when(jnp.logical_not(bottom))(lambda: send_rows(SOUTH, south, NORTH, False, 0))
    pl.when(top)(lambda: send_rows(NORTH, north, NORTH, True, 0))
    pl.when(jnp.logical_not(top))(lambda: send_rows(NORTH, north, SOUTH, True, OWN))

    loaded(0)
    loaded(tiles - 1)
    lane = lane_of((rows, LANES))
    for edge, kept, origin in ((0, to_west, 0), (tiles - 1, to_east, LANES - 8)):
        packed = jnp.zeros((rows, LANES), jnp.float32)
        for plane in range(PLANES):
            value = field[plane, edge, pl.ds(8, rows), :]
            shift = (8 * plane - origin) % LANES
            value = pltpu.roll(value, shift, 1) if shift else value
            packed = jnp.where((lane >= 8 * plane) & (lane < 8 * plane + 8), value, packed)
        kept[...] = packed

    def side(place, slot, src, dst, device):
        return pltpu.make_async_remote_copy(
            src_ref=src, dst_ref=dst, send_sem=side_send.at[place], recv_sem=side_recv.at[slot],
            device_id=device, device_id_type=MESH,
        )

    upper, lower = pl.ds(0, 8), pl.ds(8 + rows, 8)
    side(0, 1, to_east, west_in.at[pl.ds(8, rows), :], east).start()
    side(1, 0, to_west, east_in.at[pl.ds(8, rows), :], west).start()

    def corners(way, band, src, dst, right, left):
        side(2 + 2 * way, 3 + 2 * band, to_east.at[src, :], west_in.at[dst, :], right).start()
        side(3 + 2 * way, 2 + 2 * band, to_west.at[src, :], east_in.at[dst, :], left).start()

    first_rows, last_rows = pl.ds(0, 8), pl.ds(rows - 8, 8)
    pl.when(bottom)(lambda: corners(SOUTH, SOUTH, last_rows, lower, se, sw))
    pl.when(jnp.logical_not(bottom))(lambda: corners(SOUTH, NORTH, last_rows, upper, se, sw))
    pl.when(top)(lambda: corners(NORTH, NORTH, first_rows, upper, ne, nw))
    pl.when(jnp.logical_not(top))(lambda: corners(NORTH, SOUTH, first_rows, lower, ne, nw))

    lax.fori_loop(1, tiles - 1, lambda t, c: (loaded(t), c)[1], 0)
    copies = []
    for band, src, dst in ((NORTH, 8, EXTRA), (SOUTH, 8 + rows - OWN, 0)):
        copies.append(pltpu.make_async_copy(
            field.at[:, pl.ds(0, tiles), pl.ds(src, OWN), :],
            band_field.at[band, :, pl.ds(0, tiles), pl.ds(dst, OWN), :],
            own_sem.at[band],
        ))
        copies[-1].start()

    def unpacked(plane, right, left):
        back = (LANES - 8 * plane) % LANES
        right = pltpu.roll(right, back, 1) if back else right
        left = pltpu.roll(left, (LANES - 8 - 8 * plane) % LANES, 1)
        return jnp.where(lane_of(right.shape) < LANES // 2, right, left)

    middle = pl.ds(8, rows)
    for slot, box in ((0, east_in), (1, west_in)):
        pltpu.make_async_copy(box.at[middle, :], box.at[middle, :], side_recv.at[slot]).wait()
    for plane in range(PLANES):
        value = unpacked(plane, east_in[middle, :], west_in[middle, :])
        field[plane, tiles, middle, :] = value
        band_field[NORTH, plane, tiles, pl.ds(EXTRA, OWN), :] = value[:OWN]
        band_field[SOUTH, plane, tiles, pl.ds(0, OWN), :] = value[rows - OWN :]
    for copy in copies:
        copy.wait()

    inner = Region(field, other, gain, scaled, coeff, tiles + 1)
    inner.run(
        [12 + 8 * k for k in range(rows // 8 - 1)],
        [16 + 8 * k for k in range(rows // 8 - 2)],
        smoothed, residual,
        [8 + 8 * k for k in range(rows // 8 - 2)],
    )

    for band, turned, landing, box_rows, target in ((SOUTH, bottom, OWN, lower, rows - 8), (NORTH, top, 0, upper, 0)):
        for group, (planes, count) in enumerate(((slice(0, KLON), REACH), (slice(KLON, PLANES), REACH - 1))):
            got = band_field.at[band, planes, pl.ds(0, tiles), pl.ds(landing, count), :]
            pltpu.make_async_copy(got, got, row_recv.at[band, group]).wait()
        for slot, box in ((2 + 2 * band, east_in), (3 + 2 * band, west_in)):
            pltpu.make_async_copy(box.at[box_rows, :], box.at[box_rows, :], side_recv.at[slot]).wait()
        for plane in range(PLANES):
            band_field[band, plane, tiles, pl.ds(landing, 8), :] = unpacked(plane, east_in[box_rows, :], west_in[box_rows, :])

        @pl.when(turned)
        def _():
            def tile(t):
                block = band_field[band, :, t, pl.ds(landing, 8), :]
                band_field[band, :, t, pl.ds(landing, 8), :] = flipped(block)

            each_tile(tiles + 1, tile)

        edge = Region(
            band_field.at[band], band_other.at[band], band_gain.at[band], band_scaled.at[band], band_coeff.at[band], tiles + 1
        )
        edge.run([4, 12], [8], smoothed, residual, [target])

    for way in (SOUTH, NORTH):
        for group, (planes, count) in enumerate(((slice(0, KLON), REACH), (slice(KLON, PLANES), REACH - 1))):
            sent = band_field.at[way, planes, pl.ds(0, tiles), pl.ds(0, count), :]
            pltpu.make_async_copy(sent, sent, row_send.at[way, group]).wait()
        for place, box in ((2 + 2 * way, to_east), (3 + 2 * way, to_west)):
            pltpu.make_async_copy(box.at[first_rows, :], box.at[first_rows, :], side_send.at[place]).wait()
    for place, box in ((0, to_east), (1, to_west)):
        pltpu.make_async_copy(box, box, side_send.at[place]).wait()


def solution(mesh):
    bands, sectors = mesh.shape["lat"], mesh.shape["lon"]

    def on_device(right_side, start, absorb, kappa_lat, kappa_lon):
        levels, rows, columns = start.shape
        tiles = columns // LANES + 1
        deep = rows + 16

        def region(*shape):
            return [
                pltpu.VMEM(lead + (tiles,) + shape[-1:] + (LANES,), jnp.float32)
                for lead in ((*shape[:-1], PLANES),) + ((*shape[:-1], 4),) * 4
            ]

        out = pltpu.VMEM(start.shape, jnp.float32)
        return pl.pallas_call(
            functools.partial(kernel, bands, sectors),
            out_shape=(out, out),
            in_specs=[pl.BlockSpec(memory_space=pltpu.HBM)] * 5,
            out_specs=[pl.BlockSpec(memory_space=pltpu.VMEM)] * 2,
            scratch_shapes=region(deep) + region(2, OWN + EXTRA) + [
                pltpu.VMEM((rows, LANES), jnp.float32),
                pltpu.VMEM((rows, LANES), jnp.float32),
                pltpu.VMEM((deep, LANES), jnp.float32),
                pltpu.VMEM((deep, LANES), jnp.float32),
                pltpu.SemaphoreType.DMA((tiles - 1,)),
                pltpu.SemaphoreType.DMA((2,)),
                pltpu.SemaphoreType.DMA((2, 2)),
                pltpu.SemaphoreType.DMA((2, 2)),
                pltpu.SemaphoreType.DMA((6,)),
                pltpu.SemaphoreType.DMA((6,)),
            ],
            compiler_params=pltpu.CompilerParams(
                collective_id=0, has_side_effects=True, vmem_limit_bytes=62 * 1024 * 1024
            ),
        )(right_side, start, absorb, kappa_lat, kappa_lon)

    field = P(None, "lat", "lon")
    return jax.shard_map(
        on_device,
        mesh=mesh,
        in_specs=(field, field, field, P("lat", "lon"), P("lat", "lon")),
        out_specs=(field, field),
        check_vma=False,
    )
```

time: 156 us -> 33.7 us (0.22)
  the two profiles are of different devices: /device:TPU:14 before, /device:TPU:8 now
where the time goes in v1:
time: 33.7 us; the launch traced here: 33.6 us
  Pallas kernels  31.1 us (92%)
  local copies, waits for them, and re-layouts  1.85 us (5%)
  between operations  0.64 us (2%)
    pallas_call x1, Pallas kernels, on_device(): pl.pallas_call(functools.partial(kernel, bands, sectors), out_shape=(out,...  31.1 us
    unnamed x2, local copies, waits for them, and re-layouts  1.85 us

profile of v1, /device:TPU:8, one launch (start us, length us, event | category | flops | bytes accessed | tf_op | source)
XLA Modules:
  0.0 33.6 jit_solution(14976784569783039602)
XLA Ops:
  0.6 31.1 %shard_map.68 = (f32[4,64,896]{2,1,0:T(8,128)S(1)}, f32[4,64,896]{2,1,0:T(8,128)S(1)}) custom-call(f32[4,64,896]{2,1,0:T(8,128)} %right_ref.1, f32[4,64,896]{2,1,0:T(8,128)} %start_ref.1, f32[4,64,896]{2,1,0:T(8,128)} %absorb_ref.1, f32[64,896]{1,0:T(8,128)} %klat_ref.1, f32[64,896]{1,0:T(8,128)} %klon_ref.1), custom_call_target="tpu_custom_call" | custom-call | tf_op jit(solution)/shard_map/pallas_call | solution.py:321
  31.7 0.9 %copy.9 = f32[4,64,896]{2,1,0:T(8,128)} copy(f32[4,64,896]{2,1,0:T(8,128)S(1)} %get-tuple-element.2) | data formatting | bytes 1835008
  32.7 0.9 %copy.10 = f32[4,64,896]{2,1,0:T(8,128)} copy(f32[4,64,896]{2,1,0:T(8,128)S(1)} %get-tuple-element.3) | data formatting | bytes 1835008

commit v2 on v1

--- a/solution.py
+++ b/solution.py
@@ -10,6 +10,9 @@
 SWEEPS = 4
 THETA = 1.05
 DELTA = 0.95
+
+INNER_CHUNK, INNER_UNROLL, INNER_END = 8, 2, 1
+BAND_CHUNK, BAND_UNROLL, BAND_END = 8, 4, 7
 
 MESH = pl.DeviceIdType.MESH
 LANES = 128
@@ -45,37 +48,42 @@
     return pltpu.roll(jnp.where(lane_of(here.shape) == 0, right, here), LANES - 1, axis)
 
 
-def each_tile(count, body):
+def each_tile(count, body, unroll=1):
     def step(t, carry):
         body(t)
         return carry
 
-    lax.fori_loop(0, count, step, 0)
+    lax.fori_loop(0, count, step, 0, unroll=unroll)
+
+
+def chunks(first, rows, most):
+    return [(first + place, min(most, rows - place)) for place in range(0, rows, most)]
 
 
 class Region:
-    def __init__(self, field, other, gain, scaled, coeff, tiles):
+    def __init__(self, field, other, gain, scaled, coeff, tiles, unroll, unroll_end):
+        self.unroll, self.unroll_end = unroll, unroll_end
         self.field, self.other, self.gain, self.scaled, self.coeff, self.tiles = field, other, gain, scaled, coeff, tiles
 
     def around(self, t):
         return lax.rem(t + self.tiles - 1, self.tiles), lax.rem(t + 1, self.tiles)
 
-    def coupling(self, x, t, first, cn, cs, cw, ce):
+    def coupling(self, x, t, first, count, cn, cs, cw, ce):
         west, east = self.around(t)
-        rows = pl.ds(first, 8)
+        rows = pl.ds(first, count)
         here = x[0:4, t, rows, :]
-        total = cn * x[0:4, t, pl.ds(first - 1, 8), :] + cs * x[0:4, t, pl.ds(first + 1, 8), :]
+        total = cn * x[0:4, t, pl.ds(first - 1, count), :] + cs * x[0:4, t, pl.ds(first + 1, count), :]
         total += cw * from_west(x[0:4, west, rows, :], here) + ce * from_east(x[0:4, east, rows, :], here)
         return here, total
 
     def opening(self, starts):
         def tile(t):
             west, east = self.around(t)
-            for first in starts:
-                rows = pl.ds(first, 8)
+            for first, count in starts:
+                rows = pl.ds(first, count)
                 kap = self.field[KLAT, t, rows, :]
-                cn = 0.5 * (kap + self.field[KLAT, t, pl.ds(first - 1, 8), :])
-                cs = 0.5 * (kap + self.field[KLAT, t, pl.ds(first + 1, 8), :])
+                cn = 0.5 * (kap + self.field[KLAT, t, pl.ds(first - 1, count), :])
+                cs = 0.5 * (kap + self.field[KLAT, t, pl.ds(first + 1, count), :])
                 kap = self.field[KLON, t, rows, :]
                 cw = 0.5 * (kap + from_west(self.field[KLON, west, rows, :], kap))
                 ce = 0.5 * (kap + from_east(self.field[KLON, east, rows, :], kap))
@@ -85,34 +93,34 @@
                 scaled = self.field[RIGHT : RIGHT + 4, t, rows, :] * gain
                 self.gain[:, t, rows, :] = gain
                 self.scaled[:, t, rows, :] = scaled
-                here, total = self.coupling(self.field, t, first, cn, cs, cw, ce)
+                here, total = self.coupling(self.field, t, first, count, cn, cs, cw, ce)
                 self.other[:, t, rows, :] = here + (scaled - here + gain * total) * (1.0 / THETA)
 
-        each_tile(self.tiles, tile)
+        each_tile(self.tiles, tile, self.unroll)
 
     def sweep(self, now, before, starts, keep, push):
         def tile(t):
-            for first in starts:
-                rows = pl.ds(first, 8)
+            for first, count in starts:
+                rows = pl.ds(first, count)
                 cn, cs, cw, ce = (self.coeff[place, t, rows, :] for place in range(4))
-                here, total = self.coupling(now, t, first, cn, cs, cw, ce)
+                here, total = self.coupling(now, t, first, count, cn, cs, cw, ce)
                 change = push * (self.scaled[:, t, rows, :] + self.gain[:, t, rows, :] * total)
                 before[0:4, t, rows, :] = (1.0 + keep - push) * here - keep * before[0:4, t, rows, :] + change
 
-        each_tile(self.tiles, tile)
+        each_tile(self.tiles, tile, self.unroll)
 
     def closing(self, x, starts, smoothed, residual, targets):
         def tile(t):
             columns = pl.ds(pl.multiple_of(t * LANES, LANES), LANES)
-            for first, target in zip(starts, targets):
-                rows = pl.ds(first, 8)
+            for (first, count), target in zip(starts, targets):
+                rows = pl.ds(first, count)
                 cn, cs, cw, ce = (self.coeff[place, t, rows, :] for place in range(4))
-                here, total = self.coupling(x, t, first, cn, cs, cw, ce)
+                here, total = self.coupling(x, t, first, count, cn, cs, cw, ce)
                 diag = self.field[ABSORB : ABSORB + 4, t, rows, :] + (cn + cs + cw + ce)
-                smoothed[:, pl.ds(target, 8), columns] = here
-                residual[:, pl.ds(target, 8), columns] = self.field[RIGHT : RIGHT + 4, t, rows, :] - (diag * here - total)
-
-        each_tile(self.tiles - 1, tile)
+                smoothed[:, pl.ds(target, count), columns] = here
+                residual[:, pl.ds(target, count), columns] = self.field[RIGHT : RIGHT + 4, t, rows, :] - (diag * here - total)
+
+        each_tile(self.tiles - 1, tile, self.unroll_end)
 
     def run(self, starts, ends, smoothed, residual, targets):
         self.opening(starts)
@@ -135,8 +143,8 @@
     bands, sectors, right_ref, start_ref, absorb_ref, klat_ref, klon_ref, smoothed, residual,
     field, other, gain, scaled, coeff,
     band_field, band_other, band_gain, band_scaled, band_coeff,
-    to_west, to_east, east_in, west_in,
-    load_sem, own_sem, row_send, row_recv, side_send, side_recv,
+    rows_in, to_west, to_east, east_in, west_in,
+    load_sem, own_sem, row_send, row_recv, side_send, side_recv, north_in,
 ):
     rows = right_ref.shape[1]
     tiles = right_ref.shape[2] // LANES
@@ -154,9 +162,16 @@
     north, south, east, west = at(la_n, lo_n), at(la_s, lo_s), at(la, lo + 1), at(la, lo - 1)
     ne, nw, se, sw = at(la_n, lo_n + 1), at(la_n, lo_n - 1), at(la_s, lo_s + 1), at(la_s, lo_s - 1)
 
+    seam = bands // 2
+    above_seam, at_seam = la == seam - 1, la == seam
     barrier = pltpu.get_barrier_semaphore()
-    for device in (north, south, east, west, ne, nw, se, sw):
-        pl.semaphore_signal(barrier, inc=1, device_id=device, device_id_type=MESH)
+
+    def tell(semaphore, *devices):
+        for device in devices:
+            pl.semaphore_signal(semaphore, inc=1, device_id=device, device_id_type=MESH)
+
+    tell(barrier, north, ne, nw, east, west)
+    pl.when(jnp.logical_not(above_seam))(lambda: tell(barrier, south, se, sw))
 
     sources = ((start_ref, START, 4), (klat_ref, KLAT, 1), (klon_ref, KLON, 1), (right_ref, RIGHT, 4), (absorb_ref, ABSORB, 4))
 
@@ -176,33 +191,28 @@
     load(0)
     load(tiles - 1)
     lax.fori_loop(1, tiles - 1, lambda t, c: (load(t), c)[1], 0)
-    pl.semaphore_wait(barrier, 8)
-
-    def send_rows(way, device, band, from_top, into):
-        def tile(t):
-            columns = pl.ds(pl.multiple_of(t * LANES, LANES), LANES)
-            for ref, plane, depth in sources:
-                count = REACH if plane < KLON else REACH - 1
-                first = 0 if from_top else rows - count
-                group = 0 if plane < KLON else 1
-                place = into if from_top else into + 8 - count
-                if depth == 1:
-                    src = ref.at[pl.ds(first, count), columns]
-                    dst = band_field.at[band, plane, t, pl.ds(place, count), :]
-                else:
-                    src = ref.at[:, pl.ds(first, count), columns]
-                    dst = band_field.at[band, plane : plane + 4, t, pl.ds(place, count), :]
-                pltpu.make_async_remote_copy(
-                    src_ref=src, dst_ref=dst, send_sem=row_send.at[way, group], recv_sem=row_recv.at[band, group],
-                    device_id=device, device_id_type=MESH,
-                ).start()
-
-        each_tile(tiles, tile)
-
-    pl.when(bottom)(lambda: send_rows(SOUTH, south, SOUTH, False, OWN))
-    pl.when(jnp.logical_not(bottom))(lambda: send_rows(SOUTH, south, NORTH, False, 0))
-    pl.when(top)(lambda: send_rows(NORTH, north, NORTH, True, 0))
-    pl.when(jnp.logical_not(top))(lambda: send_rows(NORTH, north, SOUTH, True, OWN))
+    pl.semaphore_wait(barrier, jnp.where(at_seam, 5, 8))
+
+    def send_rows(way, device, band, from_top):
+        for ref, plane, depth in sources:
+            count = REACH if plane < KLON else REACH - 1
+            first = 0 if from_top else rows - count
+            group = 0 if plane < KLON else 1
+            place = pl.ds(0 if from_top else 8 - count, count)
+            if depth == 1:
+                src, dst = ref.at[pl.ds(first, count), :], rows_in.at[band, plane, place, :]
+            else:
+                src, dst = ref.at[:, pl.ds(first, count), :], rows_in.at[band, plane : plane + 4, place, :]
+            pltpu.make_async_remote_copy(
+                src_ref=src, dst_ref=dst, send_sem=row_send.at[way, group], recv_sem=row_recv.at[band, group],
+                device_id=device, device_id_type=MESH,
+            ).start()
+
+    band_s, band_n = jnp.where(bottom, SOUTH, NORTH), jnp.where(top, NORTH, SOUTH)
+    pl.when(above_seam)(lambda: tell(north_in, south, se, sw))
+    send_rows(SOUTH, south, band_s, False)
+
+    pl.when(jnp.logical_not(at_seam))(lambda: send_rows(NORTH, north, band_n, True))
 
     loaded(0)
     loaded(tiles - 1)
@@ -231,11 +241,13 @@
         side(3 + 2 * way, 2 + 2 * band, to_west.at[src, :], east_in.at[dst, :], left).start()
 
     first_rows, last_rows = pl.ds(0, 8), pl.ds(rows - 8, 8)
-    pl.when(bottom)(lambda: corners(SOUTH, SOUTH, last_rows, lower, se, sw))
-    pl.when(jnp.logical_not(bottom))(lambda: corners(SOUTH, NORTH, last_rows, upper, se, sw))
-    pl.when(top)(lambda: corners(NORTH, NORTH, first_rows, upper, ne, nw))
-    pl.when(jnp.logical_not(top))(lambda: corners(NORTH, SOUTH, first_rows, lower, ne, nw))
-
+    def corners(way, band, src, right, left):
+        dst = pl.ds(pl.multiple_of(band * (8 + rows), 8), 8)
+        side(2 + 2 * way, 3 + 2 * band, to_east.at[src, :], west_in.at[dst, :], right).start()
+        side(3 + 2 * way, 2 + 2 * band, to_west.at[src, :], east_in.at[dst, :], left).start()
+
+    corners(SOUTH, band_s, last_rows, se, sw)
+    pl.when(jnp.logical_not(at_seam))(lambda: corners(NORTH, band_n, first_rows, ne, nw))
     lax.fori_loop(1, tiles - 1, lambda t, c: (loaded(t), c)[1], 0)
     copies = []
     for band, src, dst in ((NORTH, 8, EXTRA), (SOUTH, 8 + rows - OWN, 0)):
@@ -263,39 +275,56 @@
     for copy in copies:
         copy.wait()
 
-    inner = Region(field, other, gain, scaled, coeff, tiles + 1)
+    inner = Region(field, other, gain, scaled, coeff, tiles + 1, INNER_UNROLL, INNER_END)
     inner.run(
-        [12 + 8 * k for k in range(rows // 8 - 1)],
-        [16 + 8 * k for k in range(rows // 8 - 2)],
+        chunks(12, rows - 8, INNER_CHUNK),
+        chunks(16, rows - 16, INNER_CHUNK),
         smoothed, residual,
-        [8 + 8 * k for k in range(rows // 8 - 2)],
+        [first - 8 for first, _ in chunks(16, rows - 16, INNER_CHUNK)],
     )
 
     for band, turned, landing, box_rows, target in ((SOUTH, bottom, OWN, lower, rows - 8), (NORTH, top, 0, upper, 0)):
+        if band == NORTH:
+
+            @pl.when(at_seam)
+            def _():
+                pl.semaphore_wait(north_in, 3)
+                send_rows(NORTH, north, band_n, True)
+                corners(NORTH, band_n, first_rows, ne, nw)
+
         for group, (planes, count) in enumerate(((slice(0, KLON), REACH), (slice(KLON, PLANES), REACH - 1))):
-            got = band_field.at[band, planes, pl.ds(0, tiles), pl.ds(landing, count), :]
+            got = rows_in.at[band, planes, pl.ds(0, count), :]
             pltpu.make_async_copy(got, got, row_recv.at[band, group]).wait()
         for slot, box in ((2 + 2 * band, east_in), (3 + 2 * band, west_in)):
             pltpu.make_async_copy(box.at[box_rows, :], box.at[box_rows, :], side_recv.at[slot]).wait()
         for plane in range(PLANES):
             band_field[band, plane, tiles, pl.ds(landing, 8), :] = unpacked(plane, east_in[box_rows, :], west_in[box_rows, :])
 
+        def settle(order):
+            def tile(t):
+                columns = pl.ds(pl.multiple_of(t * LANES, LANES), LANES)
+                band_field[band, :, t, pl.ds(landing, 8), :] = order(rows_in[band, :, :, columns])
+
+            each_tile(tiles, tile)
+
         @pl.when(turned)
         def _():
-            def tile(t):
-                block = band_field[band, :, t, pl.ds(landing, 8), :]
-                band_field[band, :, t, pl.ds(landing, 8), :] = flipped(block)
-
-            each_tile(tiles + 1, tile)
+            settle(flipped)
+            block = band_field[band, :, tiles, pl.ds(landing, 8), :]
+            band_field[band, :, tiles, pl.ds(landing, 8), :] = flipped(block)
+
+        @pl.when(jnp.logical_not(turned))
+        def _():
+            settle(lambda block: block)
 
         edge = Region(
-            band_field.at[band], band_other.at[band], band_gain.at[band], band_scaled.at[band], band_coeff.at[band], tiles + 1
+            band_field.at[band], band_other.at[band], band_gain.at[band], band_scaled.at[band], band_coeff.at[band], tiles + 1, BAND_UNROLL, BAND_END
         )
-        edge.run([4, 12], [8], smoothed, residual, [target])
+        edge.run(chunks(4, 16, BAND_CHUNK), [(8, 8)], smoothed, residual, [target])
 
     for way in (SOUTH, NORTH):
         for group, (planes, count) in enumerate(((slice(0, KLON), REACH), (slice(KLON, PLANES), REACH - 1))):
-            sent = band_field.at[way, planes, pl.ds(0, tiles), pl.ds(0, count), :]
+            sent = rows_in.at[way, planes, pl.ds(0, count), :]
             pltpu.make_async_copy(sent, sent, row_send.at[way, group]).wait()
         for place, box in ((2 + 2 * way, to_east), (3 + 2 * way, to_west)):
             pltpu.make_async_copy(box.at[first_rows, :], box.at[first_rows, :], side_send.at[place]).wait()
@@ -324,6 +353,7 @@
             in_specs=[pl.BlockSpec(memory_space=pltpu.HBM)] * 5,
             out_specs=[pl.BlockSpec(memory_space=pltpu.VMEM)] * 2,
             scratch_shapes=region(deep) + region(2, OWN + EXTRA) + [
+                pltpu.VMEM((2, PLANES, 8, columns), jnp.float32),
                 pltpu.VMEM((rows, LANES), jnp.float32),
                 pltpu.VMEM((rows, LANES), jnp.float32),
                 pltpu.VMEM((deep, LANES), jnp.float32),
@@ -334,6 +364,7 @@
                 pltpu.SemaphoreType.DMA((2, 2)),
                 pltpu.SemaphoreType.DMA((6,)),
                 pltpu.SemaphoreType.DMA((6,)),
+                pltpu.SemaphoreType.REGULAR,
             ],
             compiler_params=pltpu.CompilerParams(
                 collective_id=0, has_side_effects=True, vmem_limit_bytes=62 * 1024 * 1024

time: 33.7 us -> 24.8 us (0.74)
  the two profiles are of different devices: /device:TPU:8 before, /device:TPU:1 now
where the time goes in v2:
time: 24.8 us; the launch traced here: 24.7 us
  Pallas kernels  22.2 us (90%)
  local copies, waits for them, and re-layouts  1.85 us (7%)
  between operations  0.64 us (3%)
    pallas_call x1, Pallas kernels, on_device(): pl.pallas_call(functools.partial(kernel, bands, sectors), out_shape=(out,...  22.2 us
    unnamed x2, local copies, waits for them, and re-layouts  1.85 us

profile of v2, /device:TPU:1, one launch (start us, length us, event | category | flops | bytes accessed | tf_op | source)
XLA Modules:
  0.0 24.7 jit_solution(9483878236828267558)
XLA Ops:
  0.6 22.2 %shard_map.68 = (f32[4,64,896]{2,1,0:T(8,128)S(1)}, f32[4,64,896]{2,1,0:T(8,128)S(1)}) custom-call(f32[4,64,896]{2,1,0:T(8,128)} %right_ref.1, f32[4,64,896]{2,1,0:T(8,128)} %start_ref.1, f32[4,64,896]{2,1,0:T(8,128)} %absorb_ref.1, f32[64,896]{1,0:T(8,128)} %klat_ref.1, f32[64,896]{1,0:T(8,128)} %klon_ref.1), custom_call_target="tpu_custom_call" | custom-call | tf_op jit(solution)/shard_map/pallas_call | solution.py:350
  22.8 0.9 %copy.9 = f32[4,64,896]{2,1,0:T(8,128)} copy(f32[4,64,896]{2,1,0:T(8,128)S(1)} %get-tuple-element.2) | data formatting | bytes 1835008
  23.7 0.9 %copy.10 = f32[4,64,896]{2,1,0:T(8,128)} copy(f32[4,64,896]{2,1,0:T(8,128)S(1)} %get-tuple-element.3) | data formatting | bytes 1835008

commit v3 on v2

--- a/solution.py
+++ b/solution.py
@@ -11,8 +11,8 @@
 THETA = 1.05
 DELTA = 0.95
 
-INNER_CHUNK, INNER_UNROLL, INNER_END = 8, 2, 1
-BAND_CHUNK, BAND_UNROLL, BAND_END = 8, 4, 7
+INNER_CHUNK, INNER_UNROLL, INNER_END = 8, 1, 1
+BAND_CHUNK, BAND_UNROLL, BAND_END = 8, 8, 7
 
 MESH = pl.DeviceIdType.MESH
 LANES = 128
@@ -109,26 +109,40 @@
 
         each_tile(self.tiles, tile, self.unroll)
 
-    def closing(self, x, starts, smoothed, residual, targets):
+    def finished(self, x, t, first, count):
+        rows = pl.ds(first, count)
+        cn, cs, cw, ce = (self.coeff[place, t, rows, :] for place in range(4))
+        here, total = self.coupling(x, t, first, count, cn, cs, cw, ce)
+        diag = self.field[ABSORB : ABSORB + 4, t, rows, :] + (cn + cs + cw + ce)
+        return here, self.field[RIGHT : RIGHT + 4, t, rows, :] - (diag * here - total)
+
+    def closing(self, x, starts, smoothed, residual, targets, written):
         def tile(t):
             columns = pl.ds(pl.multiple_of(t * LANES, LANES), LANES)
             for (first, count), target in zip(starts, targets):
-                rows = pl.ds(first, count)
-                cn, cs, cw, ce = (self.coeff[place, t, rows, :] for place in range(4))
-                here, total = self.coupling(x, t, first, count, cn, cs, cw, ce)
-                diag = self.field[ABSORB : ABSORB + 4, t, rows, :] + (cn + cs + cw + ce)
+                here, left = self.finished(x, t, first, count)
                 smoothed[:, pl.ds(target, count), columns] = here
-                residual[:, pl.ds(target, count), columns] = self.field[RIGHT : RIGHT + 4, t, rows, :] - (diag * here - total)
-
-        each_tile(self.tiles - 1, tile, self.unroll_end)
-
-    def run(self, starts, ends, smoothed, residual, targets):
+                residual[:, pl.ds(target, count), columns] = left
+
+        each_tile(written, tile, self.unroll_end)
+
+    def closing_sides(self, x, starts, smoothed, residual, targets, last):
+        for t, column, outer in ((0, last, True), (2, 0, False)):
+            columns = pl.ds(column * LANES, LANES)
+            for (first, count), target in zip(starts, targets):
+                near = lane_of((4, count, LANES)) < LANES // 2
+                near = jnp.logical_not(near) if outer else near
+                for ref, value in zip((smoothed, residual), self.finished(x, t, first, count)):
+                    place = (slice(None), pl.ds(target, count), columns)
+                    ref[place] = jnp.where(near, value, ref[place])
+
+    def sweeps(self, starts):
         self.opening(starts)
         now, before = self.other, self.field
         for keep, push in sweep_factors():
             self.sweep(now, before, starts, keep, push)
             now, before = before, now
-        self.closing(now, ends, smoothed, residual, targets)
+        return now
 
 
 def flipped(block):
@@ -143,6 +157,7 @@
     bands, sectors, right_ref, start_ref, absorb_ref, klat_ref, klon_ref, smoothed, residual,
     field, other, gain, scaled, coeff,
     band_field, band_other, band_gain, band_scaled, band_coeff,
+    side_field, side_other, side_gain, side_scaled, side_coeff,
     rows_in, to_west, to_east, east_in, west_in,
     load_sem, own_sem, row_send, row_recv, side_send, side_recv, north_in,
 ):
@@ -163,15 +178,16 @@
     ne, nw, se, sw = at(la_n, lo_n + 1), at(la_n, lo_n - 1), at(la_s, lo_s + 1), at(la_s, lo_s - 1)
 
     seam = bands // 2
-    above_seam, at_seam = la == seam - 1, la == seam
+    two_above, above_seam, at_seam = la == seam - 2, la == seam - 1, la == seam
     barrier = pltpu.get_barrier_semaphore()
 
     def tell(semaphore, *devices):
         for device in devices:
             pl.semaphore_signal(semaphore, inc=1, device_id=device, device_id_type=MESH)
 
-    tell(barrier, north, ne, nw, east, west)
-    pl.when(jnp.logical_not(above_seam))(lambda: tell(barrier, south, se, sw))
+    tell(barrier, north, ne, nw)
+    pl.when(jnp.logical_not(above_seam))(lambda: tell(barrier, east, west))
+    pl.when(jnp.logical_not(above_seam | two_above))(lambda: tell(barrier, south, se, sw))
 
     sources = ((start_ref, START, 4), (klat_ref, KLAT, 1), (klon_ref, KLON, 1), (right_ref, RIGHT, 4), (absorb_ref, ABSORB, 4))
 
@@ -191,7 +207,7 @@
     load(0)
     load(tiles - 1)
     lax.fori_loop(1, tiles - 1, lambda t, c: (load(t), c)[1], 0)
-    pl.semaphore_wait(barrier, jnp.where(at_seam, 5, 8))
+    pl.semaphore_wait(barrier, jnp.where(above_seam, 3, jnp.where(at_seam, 5, 8)))
 
     def send_rows(way, device, band, from_top):
         for ref, plane, depth in sources:
@@ -210,8 +226,10 @@
 
     band_s, band_n = jnp.where(bottom, SOUTH, NORTH), jnp.where(top, NORTH, SOUTH)
     pl.when(above_seam)(lambda: tell(north_in, south, se, sw))
+    pl.when(two_above)(lambda: tell(north_in, south))
     send_rows(SOUTH, south, band_s, False)
 
+    pl.when(above_seam)(lambda: pl.semaphore_wait(north_in, 1))
     pl.when(jnp.logical_not(at_seam))(lambda: send_rows(NORTH, north, band_n, True))
 
     loaded(0)
@@ -236,10 +254,6 @@
     side(0, 1, to_east, west_in.at[pl.ds(8, rows), :], east).start()
     side(1, 0, to_west, east_in.at[pl.ds(8, rows), :], west).start()
 
-    def corners(way, band, src, dst, right, left):
-        side(2 + 2 * way, 3 + 2 * band, to_east.at[src, :], west_in.at[dst, :], right).start()
-        side(3 + 2 * way, 2 + 2 * band, to_west.at[src, :], east_in.at[dst, :], left).start()
-
     first_rows, last_rows = pl.ds(0, 8), pl.ds(rows - 8, 8)
     def corners(way, band, src, right, left):
         dst = pl.ds(pl.multiple_of(band * (8 + rows), 8), 8)
@@ -257,6 +271,11 @@
             own_sem.at[band],
         ))
         copies[-1].start()
+    for place, t in ((0, tiles - 1), (2, 0)):
+        copies.append(pltpu.make_async_copy(
+            field.at[:, t, pl.ds(8, rows), :], side_field.at[:, place, pl.ds(8, rows), :], own_sem.at[2 + place // 2]
+        ))
+        copies[-1].start()
 
     def unpacked(plane, right, left):
         back = (LANES - 8 * plane) % LANES
@@ -264,24 +283,25 @@
         left = pltpu.roll(left, (LANES - 8 - 8 * plane) % LANES, 1)
         return jnp.where(lane_of(right.shape) < LANES // 2, right, left)
 
+    for copy in copies:
+        copy.wait()
+
+    starts, ends = chunks(12, rows - 8, INNER_CHUNK), chunks(16, rows - 16, INNER_CHUNK)
+    targets = [first - 8 for first, _ in ends]
+    inner = Region(field, other, gain, scaled, coeff, tiles, INNER_UNROLL, INNER_END)
+    inner.closing(inner.sweeps(starts), ends, smoothed, residual, targets, tiles)
+
     middle = pl.ds(8, rows)
     for slot, box in ((0, east_in), (1, west_in)):
         pltpu.make_async_copy(box.at[middle, :], box.at[middle, :], side_recv.at[slot]).wait()
     for plane in range(PLANES):
         value = unpacked(plane, east_in[middle, :], west_in[middle, :])
-        field[plane, tiles, middle, :] = value
+        side_field[plane, 1, middle, :] = value
         band_field[NORTH, plane, tiles, pl.ds(EXTRA, OWN), :] = value[:OWN]
         band_field[SOUTH, plane, tiles, pl.ds(0, OWN), :] = value[rows - OWN :]
-    for copy in copies:
-        copy.wait()
-
-    inner = Region(field, other, gain, scaled, coeff, tiles + 1, INNER_UNROLL, INNER_END)
-    inner.run(
-        chunks(12, rows - 8, INNER_CHUNK),
-        chunks(16, rows - 16, INNER_CHUNK),
-        smoothed, residual,
-        [first - 8 for first, _ in chunks(16, rows - 16, INNER_CHUNK)],
-    )
+
+    sides = Region(side_field, side_other, side_gain, side_scaled, side_coeff, 3, 3, 1)
+    sides.closing_sides(sides.sweeps(starts), ends, smoothed, residual, targets, tiles - 1)
 
     for band, turned, landing, box_rows, target in ((SOUTH, bottom, OWN, lower, rows - 8), (NORTH, top, 0, upper, 0)):
         if band == NORTH:
@@ -320,7 +340,7 @@
         edge = Region(
             band_field.at[band], band_other.at[band], band_gain.at[band], band_scaled.at[band], band_coeff.at[band], tiles + 1, BAND_UNROLL, BAND_END
         )
-        edge.run(chunks(4, 16, BAND_CHUNK), [(8, 8)], smoothed, residual, [target])
+        edge.closing(edge.sweeps(chunks(4, OWN, BAND_CHUNK)), [(8, 8)], smoothed, residual, [target], tiles)
 
     for way in (SOUTH, NORTH):
         for group, (planes, count) in enumerate(((slice(0, KLON), REACH), (slice(KLON, PLANES), REACH - 1))):
@@ -340,7 +360,7 @@
         tiles = columns // LANES + 1
         deep = rows + 16
 
-        def region(*shape):
+        def region(tiles, *shape):
             return [
                 pltpu.VMEM(lead + (tiles,) + shape[-1:] + (LANES,), jnp.float32)
                 for lead in ((*shape[:-1], PLANES),) + ((*shape[:-1], 4),) * 4
@@ -352,14 +372,14 @@
             out_shape=(out, out),
             in_specs=[pl.BlockSpec(memory_space=pltpu.HBM)] * 5,
             out_specs=[pl.BlockSpec(memory_space=pltpu.VMEM)] * 2,
-            scratch_shapes=region(deep) + region(2, OWN + EXTRA) + [
+            scratch_shapes=region(tiles - 1, deep) + region(tiles, 2, OWN + EXTRA) + region(3, deep) + [
                 pltpu.VMEM((2, PLANES, 8, columns), jnp.float32),
                 pltpu.VMEM((rows, LANES), jnp.float32),
                 pltpu.VMEM((rows, LANES), jnp.float32),
                 pltpu.VMEM((deep, LANES), jnp.float32),
                 pltpu.VMEM((deep, LANES), jnp.float32),
                 pltpu.SemaphoreType.DMA((tiles - 1,)),
-                pltpu.SemaphoreType.DMA((2,)),
+                pltpu.SemaphoreType.DMA((4,)),
                 pltpu.SemaphoreType.DMA((2, 2)),
                 pltpu.SemaphoreType.DMA((2, 2)),
                 pltpu.SemaphoreType.DMA((6,)),

time: 24.8 us -> 21.3 us (0.86)
  the two profiles are of different devices: /device:TPU:1 before, /device:TPU:10 now
where the time goes in v3:
time: 21.3 us; the launch traced here: 21.1 us
  Pallas kernels  18.6 us (87%)
  local copies, waits for them, and re-layouts  1.85 us (9%)
  between operations  0.64 us (3%)
    pallas_call x1, Pallas kernels, on_device(): pl.pallas_call(functools.partial(kernel, bands, sectors), out_shape=(out,...  18.6 us
    unnamed x2, local copies, waits for them, and re-layouts  1.85 us

profile of v3, /device:TPU:10, one launch (start us, length us, event | category | flops | bytes accessed | tf_op | source)
XLA Modules:
  0.0 21.1 jit_solution(8355870163395819432)
XLA Ops:
  0.6 18.6 %shard_map.68 = (f32[4,64,896]{2,1,0:T(8,128)S(1)}, f32[4,64,896]{2,1,0:T(8,128)S(1)}) custom-call(f32[4,64,896]{2,1,0:T(8,128)} %right_ref.1, f32[4,64,896]{2,1,0:T(8,128)} %start_ref.1, f32[4,64,896]{2,1,0:T(8,128)} %absorb_ref.1, f32[64,896]{1,0:T(8,128)} %klat_ref.1, f32[64,896]{1,0:T(8,128)} %klon_ref.1), custom_call_target="tpu_custom_call" | custom-call | tf_op jit(solution)/shard_map/pallas_call | solution.py:370
  19.3 0.9 %copy.9 = f32[4,64,896]{2,1,0:T(8,128)} copy(f32[4,64,896]{2,1,0:T(8,128)S(1)} %get-tuple-element.2) | data formatting | bytes 1835008
  20.2 0.9 %copy.10 = f32[4,64,896]{2,1,0:T(8,128)} copy(f32[4,64,896]{2,1,0:T(8,128)S(1)} %get-tuple-element.3) | data formatting | bytes 1835008

commit v4 on v3

--- a/solution.py
+++ b/solution.py
@@ -207,7 +207,6 @@
     load(0)
     load(tiles - 1)
     lax.fori_loop(1, tiles - 1, lambda t, c: (load(t), c)[1], 0)
-    pl.semaphore_wait(barrier, jnp.where(above_seam, 3, jnp.where(at_seam, 5, 8)))
 
     def send_rows(way, device, band, from_top):
         for ref, plane, depth in sources:
@@ -225,12 +224,12 @@
             ).start()
 
     band_s, band_n = jnp.where(bottom, SOUTH, NORTH), jnp.where(top, NORTH, SOUTH)
-    pl.when(above_seam)(lambda: tell(north_in, south, se, sw))
-    pl.when(two_above)(lambda: tell(north_in, south))
-    send_rows(SOUTH, south, band_s, False)
-
-    pl.when(above_seam)(lambda: pl.semaphore_wait(north_in, 1))
-    pl.when(jnp.logical_not(at_seam))(lambda: send_rows(NORTH, north, band_n, True))
+
+    @pl.when(above_seam)
+    def _():
+        pl.semaphore_wait(barrier, 3)
+        tell(north_in, south, se, sw)
+        send_rows(SOUTH, south, band_s, False)
 
     loaded(0)
     loaded(tiles - 1)
@@ -251,17 +250,29 @@
         )
 
     upper, lower = pl.ds(0, 8), pl.ds(8 + rows, 8)
-    side(0, 1, to_east, west_in.at[pl.ds(8, rows), :], east).start()
-    side(1, 0, to_west, east_in.at[pl.ds(8, rows), :], west).start()
-
     first_rows, last_rows = pl.ds(0, 8), pl.ds(rows - 8, 8)
+
     def corners(way, band, src, right, left):
         dst = pl.ds(pl.multiple_of(band * (8 + rows), 8), 8)
         side(2 + 2 * way, 3 + 2 * band, to_east.at[src, :], west_in.at[dst, :], right).start()
         side(3 + 2 * way, 2 + 2 * band, to_west.at[src, :], east_in.at[dst, :], left).start()
 
-    corners(SOUTH, band_s, last_rows, se, sw)
+    pl.when(above_seam)(lambda: corners(SOUTH, band_s, last_rows, se, sw))
+
+    @pl.when(jnp.logical_not(above_seam))
+    def _():
+        pl.semaphore_wait(barrier, jnp.where(at_seam, 5, 8))
+
+    pl.when(two_above)(lambda: tell(north_in, south))
+    pl.when(above_seam)(lambda: pl.semaphore_wait(north_in, 1))
+
+    side(0, 1, to_east, west_in.at[pl.ds(8, rows), :], east).start()
+    side(1, 0, to_west, east_in.at[pl.ds(8, rows), :], west).start()
+
+    pl.when(jnp.logical_not(above_seam))(lambda: corners(SOUTH, band_s, last_rows, se, sw))
     pl.when(jnp.logical_not(at_seam))(lambda: corners(NORTH, band_n, first_rows, ne, nw))
+    pl.when(jnp.logical_not(above_seam))(lambda: send_rows(SOUTH, south, band_s, False))
+    pl.when(jnp.logical_not(at_seam))(lambda: send_rows(NORTH, north, band_n, True))
     lax.fori_loop(1, tiles - 1, lambda t, c: (loaded(t), c)[1], 0)
     copies = []
     for band, src, dst in ((NORTH, 8, EXTRA), (SOUTH, 8 + rows - OWN, 0)):

time: 21.3 us -> 21 us (0.986)
  the two profiles are of different devices: /device:TPU:10 before, /device:TPU:8 now
where the time goes in v4:
time: 21 us; the launch traced here: 20.8 us
  Pallas kernels  18.3 us (87%)
  local copies, waits for them, and re-layouts  1.85 us (9%)
  between operations  0.64 us (3%)
    pallas_call x1, Pallas kernels, on_device(): pl.pallas_call(functools.partial(kernel, bands, sectors), out_shape=(out,...  18.3 us
    unnamed x2, local copies, waits for them, and re-layouts  1.85 us

profile of v4, /device:TPU:8, one launch (start us, length us, event | category | flops | bytes accessed | tf_op | source)
XLA Modules:
  0.0 20.8 jit_solution(297906813079868271)
XLA Ops:
  0.6 18.3 %shard_map.68 = (f32[4,64,896]{2,1,0:T(8,128)S(1)}, f32[4,64,896]{2,1,0:T(8,128)S(1)}) custom-call(f32[4,64,896]{2,1,0:T(8,128)} %right_ref.1, f32[4,64,896]{2,1,0:T(8,128)} %start_ref.1, f32[4,64,896]{2,1,0:T(8,128)} %absorb_ref.1, f32[64,896]{1,0:T(8,128)} %klat_ref.1, f32[64,896]{1,0:T(8,128)} %klon_ref.1), custom_call_target="tpu_custom_call" | custom-call | tf_op jit(solution)/shard_map/pallas_call | solution.py:381
  19.0 0.9 %copy.9 = f32[4,64,896]{2,1,0:T(8,128)} copy(f32[4,64,896]{2,1,0:T(8,128)S(1)} %get-tuple-element.2) | data formatting | bytes 1835008
  19.9 0.9 %copy.10 = f32[4,64,896]{2,1,0:T(8,128)} copy(f32[4,64,896]{2,1,0:T(8,128)S(1)} %get-tuple-element.3) | data formatting | bytes 1835008
